TPU v7x, 32 devices: a whole 2x2x4 slice. The times are simulated.
32 devices in a mesh: rep: 4 (over z), fsdp: 4 (over y, core), seq: 2 (over x).
Axes of the slice: x: 2, y: 2, z: 4, core: 2. Of those that a mesh axis runs over, the one named last changes fastest.
Arguments:
- tokens: bfloat16 [32, 1024, 1024], P(('rep', 'fsdp'), 'seq'), may hold values from -6 to 6
- cotangent: bfloat16 [32, 1024, 1024], P(('rep', 'fsdp'), 'seq'), may hold values from -6 to 6
- adapter_set: int32 [32], P(('rep', 'fsdp')), may hold values from 0 to 7
- image_live: int32 [32], P(('rep', 'fsdp')), may hold values from 0 to 1, as said below
- first_gain: float32 [1024], replicated, may hold values from 0.5 to 1.5
- first_shift: float32 [1024], replicated, may hold values from -2 to 2
- inproj_weight: bfloat16 [1024, 3072], P('fsdp'), may hold values from -0.1875 to 0.1875
- inproj_bias: float32 [2048], replicated, may hold values from -2 to 2
- outproj_weight: bfloat16 [1024, 1024], P('fsdp'), may hold values from -0.75 to 0.75
- outproj_bias: float32 [1024], replicated, may hold values from -2 to 2
- attend_scale: float32 [1024], replicated, may hold values from 0.5 to 1.5
- second_gain: float32 [1024], replicated, may hold values from 0.5 to 1.5
- second_shift: float32 [1024], replicated, may hold values from -2 to 2
- expand_weight: bfloat16 [1024, 4096], P('fsdp'), may hold values from -0.1875 to 0.1875
- expand_bias: float32 [4096], replicated, may hold values from -2 to 2
- shrink_weight: bfloat16 [4096, 1024], P('fsdp'), may hold values from -0.09375 to 0.09375
- shrink_bias: float32 [1024], replicated, may hold values from -2 to 2
- feedfwd_scale: float32 [1024], replicated, may hold values from 0.5 to 1.5
- inproj_first: float32 [8, 1024, 16], replicated, may hold values from -0.1875 to 0.1875
- inproj_second: float32 [8, 16, 3072], replicated, may hold values from -0.75 to 0.75
- outproj_first: float32 [8, 1024, 16], replicated, may hold values from -0.1875 to 0.1875
- outproj_second: float32 [8, 16, 1024], replicated, may hold values from -0.75 to 0.75
- expand_first: float32 [8, 1024, 16], replicated, may hold values from -0.1875 to 0.1875
- expand_second: float32 [8, 16, 4096], replicated, may hold values from -0.75 to 0.75
- shrink_first: float32 [8, 4096, 16], replicated, may hold values from -0.1875 to 0.1875
- shrink_second: float32 [8, 16, 1024], replicated, may hold values from -0.75 to 0.75
Outputs:
- block_output: bfloat16 [32, 1024, 1024], P(('rep', 'fsdp'), 'seq')
- input_grad: bfloat16 [32, 1024, 1024], P(('rep', 'fsdp'), 'seq')
- inproj_first_grad: float32 [8, 1024, 16], replicated
- inproj_second_grad: float32 [8, 16, 3072], replicated
- outproj_first_grad: float32 [8, 1024, 16], replicated
- outproj_second_grad: float32 [8, 16, 1024], replicated
- expand_first_grad: float32 [8, 1024, 16], replicated
- expand_second_grad: float32 [8, 16, 4096], replicated
- shrink_first_grad: float32 [8, 4096, 16], replicated
- shrink_second_grad: float32 [8, 16, 1024], replicated
Inputs may be any that keep to these rules, and one draw needn't show every extreme that they name: `image_live`: image slots come in groups of 2 consecutive ones, one group for each index pair of rep and fsdp; in each group the live slots come first, at least one is live, and in some group all 2 are live.
All inputs are finite; a program needn't handle non-finite values.
Results may differ from a plain program's by a relative error of at most 0.018.
The roundings to bfloat16 on the way count: a program that leaves them out, or rounds other values in their place, can miss the bound.
Values may be sent and summed in bfloat16 or wider, within the bound.
A program may use at most 320 MiB of HBM per device.

v0:
```python
import math

import jax
import jax.numpy as jnp
from jax import lax
from jax.sharding import PartitionSpec as P

HEADS = 16
HEAD_DIM = 64


epsilon = 1e-06


def layer_norm(values, gain, shift):
    center = values - jnp.mean(values, axis=-1, keepdims=True)
    spread = jnp.mean(center * center, axis=-1, keepdims=True)
    return center * lax.rsqrt(spread + epsilon) * gain + shift


def project(activation, matrix):
    return jnp.einsum("nlc,cd->nld", activation, matrix, preferred_element_type=jnp.float32)


def project_back(gradient, matrix):
    return jnp.einsum("nld,cd->nlc", gradient, matrix, preferred_element_type=jnp.float32)


def enter_rank(activation, factor):
    return jnp.einsum("nlc,ncr->nlr", activation, factor, preferred_element_type=jnp.float32)


def enter_rank_back(gradient, factor):
    return jnp.einsum("nlr,ncr->nlc", gradient, factor, preferred_element_type=jnp.float32)


def leave_rank(activation, factor):
    return jnp.einsum("nlr,nrd->nld", activation, factor, preferred_element_type=jnp.float32)


def leave_rank_back(gradient, factor):
    return jnp.einsum("nld,nrd->nlr", gradient, factor, preferred_element_type=jnp.float32)


def first_term(activation, gradient):
    return jnp.einsum("nlc,nlr->ncr", activation, gradient, preferred_element_type=jnp.float32)


def second_term(activation, gradient):
    return 2.0 * jnp.einsum(
        "nlr,nld->nrd", activation, gradient, preferred_element_type=jnp.float32
    )


def shards(
    tokens,
    cotangent,
    adapter_set,
    image_live,
    first_gain,
    first_shift,
    inproj_weight,
    inproj_bias,
    outproj_weight,
    outproj_bias,
    attend_scale,
    second_gain,
    second_shift,
    expand_weight,
    expand_bias,
    shrink_weight,
    shrink_bias,
    feedfwd_scale,
    inproj_first,
    inproj_second,
    outproj_first,
    outproj_second,
    expand_first,
    expand_second,
    shrink_first,
    shrink_second,
):
    slot_count, row_count, width = tokens.shape
    group_size = math.gcd(slot_count, max(1, 512 // row_count))
    block_count = slot_count // group_size
    set_count = inproj_first.shape[0]
    matches = adapter_set[:, None] == jnp.arange(set_count)[None, :]
    choose_low = matches.astype(jnp.bfloat16)
    choose_wide = matches.astype(jnp.float32)
    live_mask = image_live.astype(jnp.float32)[:, None, None]

    def select(table):
        table_low = table.astype(jnp.bfloat16)
        picked = jnp.einsum(
            "ns,sij->nij", choose_low, table_low, preferred_element_type=jnp.float32
        )
        return picked.astype(jnp.bfloat16)

    def fold(terms):
        return jnp.sum(choose_wide[:, :, None, None] * terms[:, None, :, :], axis=0)

    enter_first = select(inproj_first)
    enter_second = select(inproj_second)
    leave_first = select(outproj_first)
    leave_second = select(outproj_second)
    widen_first = select(expand_first)
    widen_second = select(expand_second)
    narrow_first = select(shrink_first)
    narrow_second = select(shrink_second)
    whole_inproj, whole_outproj, whole_expand, whole_shrink = (
        lax.all_gather(inproj_weight, "fsdp", axis=0, tiled=True),
        lax.all_gather(outproj_weight, "fsdp", axis=0, tiled=True),
        lax.all_gather(expand_weight, "fsdp", axis=0, tiled=True),
        lax.all_gather(shrink_weight, "fsdp", axis=0, tiled=True),
    )

    def norm_one(values):
        return layer_norm(values, first_gain, first_shift)

    def norm_two(values):
        return layer_norm(values, second_gain, second_shift)

    def gelu_exact(values):
        return jax.nn.gelu(values, approximate=False)

    values = tokens.astype(jnp.float32)
    normed_one = norm_one(values).astype(jnp.bfloat16)
    enter_low = enter_rank(normed_one, enter_first).astype(jnp.bfloat16)
    bias_full = jnp.concatenate(
        [inproj_bias[:width], jnp.zeros((width,), jnp.float32), inproj_bias[width:]]
    )
    joined = (
        project(normed_one, whole_inproj) + bias_full + 2.0 * leave_rank(enter_low, enter_second)
    )
    queries = joined[..., :width].astype(jnp.bfloat16)
    key_rows = joined[..., width : 2 * width].astype(jnp.bfloat16)
    value_rows = joined[..., 2 * width :].astype(jnp.bfloat16)
    key_all, value_all = (
        lax.all_gather(key_rows, "seq", axis=1, tiled=True),
        lax.all_gather(value_rows, "seq", axis=1, tiled=True),
    )
    length = key_all.shape[1]
    query_blocks = queries.reshape(block_count, group_size, row_count, HEADS, HEAD_DIM)
    key_blocks = key_all.reshape(block_count, group_size, length, HEADS, HEAD_DIM)
    value_blocks = value_all.reshape(block_count, group_size, length, HEADS, HEAD_DIM)

    def attend_forward(packed):
        query_part, key_part, value_part = packed
        scores = (
            jnp.einsum("gqhe,gkhe->ghqk", query_part, key_part, preferred_element_type=jnp.float32)
            * 0.125
        )
        top = jnp.max(scores, axis=-1, keepdims=True)
        expo = jnp.exp(scores - top)
        total = jnp.sum(expo, axis=-1, keepdims=True)
        attention = (expo / total).astype(jnp.bfloat16)
        mixed = jnp.einsum(
            "ghqk,gkhe->gqhe", attention, value_part, preferred_element_type=jnp.float32
        )
        return (mixed.astype(jnp.bfloat16), top[..., 0] + jnp.log(total[..., 0]))

    mixed_blocks, logsum = lax.map(attend_forward, (query_blocks, key_blocks, value_blocks))
    attended = mixed_blocks.reshape(slot_count, row_count, width)
    leave_low = enter_rank(attended, leave_first).astype(jnp.bfloat16)
    branch = (
        project(attended, whole_outproj) + outproj_bias + 2.0 * leave_rank(leave_low, leave_second)
    )
    middle = values + attend_scale * branch
    normed_two = norm_two(middle).astype(jnp.bfloat16)
    widen_low = enter_rank(normed_two, widen_first).astype(jnp.bfloat16)
    before = (
        project(normed_two, whole_expand) + expand_bias + 2.0 * leave_rank(widen_low, widen_second)
    )
    hidden = gelu_exact(before).astype(jnp.bfloat16)
    narrow_low = enter_rank(hidden, narrow_first).astype(jnp.bfloat16)
    feed = project(hidden, whole_shrink) + shrink_bias + 2.0 * leave_rank(narrow_low, narrow_second)
    result = middle + feedfwd_scale * feed
    block_output = (result * live_mask).astype(jnp.bfloat16)
    back_inproj, back_outproj, back_expand, back_shrink = (
        lax.all_gather(inproj_weight, "fsdp", axis=0, tiled=True),
        lax.all_gather(outproj_weight, "fsdp", axis=0, tiled=True),
        lax.all_gather(expand_weight, "fsdp", axis=0, tiled=True),
        lax.all_gather(shrink_weight, "fsdp", axis=0, tiled=True),
    )
    grad_res = cotangent.astype(jnp.float32) * live_mask
    grad_feed = (grad_res * feedfwd_scale).astype(jnp.bfloat16)
    narrow_second_terms = second_term(narrow_low, grad_feed)
    grad_narrow = (2.0 * leave_rank_back(grad_feed, narrow_second)).astype(jnp.bfloat16)
    grad_hidden = (
        project_back(grad_feed, back_shrink) + enter_rank_back(grad_narrow, narrow_first)
    ).astype(jnp.bfloat16)
    narrow_first_terms = first_term(hidden, grad_narrow)
    gelu_out, gelu_pull = jax.vjp(gelu_exact, before)
    grad_before = gelu_pull(grad_hidden.astype(jnp.float32))[0].astype(jnp.bfloat16)
    widen_second_terms = second_term(widen_low, grad_before)
    grad_widen = (2.0 * leave_rank_back(grad_before, widen_second)).astype(jnp.bfloat16)
    grad_normed_two = project_back(grad_before, back_expand) + enter_rank_back(
        grad_widen, widen_first
    )
    widen_first_terms = first_term(normed_two, grad_widen)
    norm_out, norm_pull = jax.vjp(norm_two, middle)
    grad_middle = grad_res + norm_pull(grad_normed_two)[0]
    grad_branch = (grad_middle * attend_scale).astype(jnp.bfloat16)
    leave_second_terms = second_term(leave_low, grad_branch)
    grad_leave = (2.0 * leave_rank_back(grad_branch, leave_second)).astype(jnp.bfloat16)
    grad_attended = (
        project_back(grad_branch, back_outproj) + enter_rank_back(grad_leave, leave_first)
    ).astype(jnp.bfloat16)
    leave_first_terms = first_term(attended, grad_leave)
    grad_blocks = grad_attended.reshape(block_count, group_size, row_count, HEADS, HEAD_DIM)

    def attend_backward(packed):
        query_part, key_part, value_part, grad_part, logsum_part = packed
        scores = (
            jnp.einsum("gqhe,gkhe->ghqk", query_part, key_part, preferred_element_type=jnp.float32)
            * 0.125
        )
        probs = jnp.exp(scores - logsum_part[..., None])
        prob_low = probs.astype(jnp.bfloat16)
        value_term = jnp.einsum(
            "ghqk,gqhe->gkhe", prob_low, grad_part, preferred_element_type=jnp.float32
        )
        grad_prob = jnp.einsum(
            "gqhe,gkhe->ghqk", grad_part, value_part, preferred_element_type=jnp.float32
        )
        inner = jnp.sum(probs * grad_prob, axis=-1, keepdims=True)
        grad_scores = (probs * (grad_prob - inner)).astype(jnp.bfloat16)
        grad_query = (
            jnp.einsum("ghqk,gkhe->gqhe", grad_scores, key_part, preferred_element_type=jnp.float32)
            * 0.125
        )
        key_term = (
            jnp.einsum(
                "ghqk,gqhe->gkhe", grad_scores, query_part, preferred_element_type=jnp.float32
            )
            * 0.125
        )
        key_term = key_term.reshape(group_size, length, width)
        value_term = value_term.reshape(group_size, length, width)
        summed_key, summed_value = (
            lax.psum_scatter(
                key_term.astype(jnp.bfloat16), "seq", scatter_dimension=1, tiled=True
            ).astype(jnp.float32),
            lax.psum_scatter(
                value_term.astype(jnp.bfloat16), "seq", scatter_dimension=1, tiled=True
            ).astype(jnp.float32),
        )
        return (
            grad_query.astype(jnp.bfloat16).reshape(group_size, row_count, width),
            summed_key.astype(jnp.bfloat16),
            summed_value.astype(jnp.bfloat16),
        )

    grad_queries, grad_keys, grad_values = lax.map(
        attend_backward, (query_blocks, key_blocks, value_blocks, grad_blocks, logsum)
    )
    grad_joined = jnp.concatenate(
        [
            grad_queries.reshape(slot_count, row_count, width),
            grad_keys.reshape(slot_count, row_count, width),
            grad_values.reshape(slot_count, row_count, width),
        ],
        axis=-1,
    )
    enter_second_terms = second_term(enter_low, grad_joined)
    grad_enter = (2.0 * leave_rank_back(grad_joined, enter_second)).astype(jnp.bfloat16)
    grad_normed_one = project_back(grad_joined, back_inproj) + enter_rank_back(
        grad_enter, enter_first
    )
    enter_first_terms = first_term(normed_one, grad_enter)
    first_out, first_pull = jax.vjp(norm_one, values)
    input_grad = (grad_middle + first_pull(grad_normed_one)[0]).astype(jnp.bfloat16)
    summed = lax.psum(
        (
            fold(enter_first_terms),
            fold(enter_second_terms),
            fold(leave_first_terms),
            fold(leave_second_terms),
            fold(widen_first_terms),
            fold(widen_second_terms),
            fold(narrow_first_terms),
            fold(narrow_second_terms),
        ),
        ("rep", "fsdp", "seq"),
    )
    return (
        block_output,
        input_grad,
        summed[0],
        summed[1],
        summed[2],
        summed[3],
        summed[4],
        summed[5],
        summed[6],
        summed[7],
    )


def solution(mesh):
    return jax.shard_map(
        shards,
        mesh=mesh,
        in_specs=(
            P(("rep", "fsdp"), "seq", None),
            P(("rep", "fsdp"), "seq", None),
            P(("rep", "fsdp")),
            P(("rep", "fsdp")),
            P(),
            P(),
            P("fsdp", None),
            P(),
            P("fsdp", None),
            P(),
            P(),
            P(),
            P(),
            P("fsdp", None),
            P(),
            P("fsdp", None),
            P(),
            P(),
            P(),
            P(),
            P(),
            P(),
            P(),
            P(),
            P(),
            P(),
        ),
        out_specs=(
            P(("rep", "fsdp"), "seq", None),
            P(("rep", "fsdp"), "seq", None),
            P(),
            P(),
            P(),
            P(),
            P(),
            P(),
            P(),
            P(),
        ),
        check_vma=False,
    )
```

profile of v0, /device:TPU:0, one launch (start us, length us, event | category | flops | bytes accessed | tf_op | source)
XLA Modules:
  0.0 970.5 jit_solution(11351822484569505173)
XLA Ops:
  15.1 43.7 %all-gather.7.cloned.1.call-done = bf16[1024,3072]{1,0:T(8,128)(2,1)} async-done(((bf16[256,3072]{1,0:T(8,128)(2,1)}), bf16[1024,3072]{1,0:T(8,128)(2,1)}) %all-gather.7.cloned.1.call-update) | async-done | bytes 6291472 | tf_op jit(solution)/shard_map/all_gather | solution.py:111
  89.4 29.2 %all-gather.17.cloned.1.call-done = bf16[4096,1024]{1,0:T(8,128)(2,1)} async-done(((bf16[1024,1024]{1,0:T(8,128)(2,1)}), bf16[4096,1024]{1,0:T(8,128)(2,1)}) %all-gather.17.cloned.1.call-update) | async-done | bytes 8388624 | tf_op jit(solution)/shard_map/all_gather | solution.py:114
  118.6 16.1 %fusion.67 = f32[2,512,4096]{2,1,0:T(8,128)} fusion(bf16[4096,1024]{1,0:T(8,128)(2,1)} %all-gather.17.cloned.1.call-done, bf16[2,512,1024]{2,1,0:T(8,128)(2,1)} %param.31, f32[2]{0:T(128)S(1)} %convert_element_type.223, f32[1024]{0:T(1024)S(1)} %copy-done.72), kind=kOutput, calls=%fused_computation.86 | convolution fusion | flops 8594128896 | bytes 27267080 | tf_op jit(solution)/shard_map/nld,cd->nlc/dot_general | solution.py:26
  134.7 42.8 %all-gather.11.cloned.1.call-done = bf16[2,1024,1024]{2,1,0:T(8,128)(2,1)} async-done(((bf16[2,512,1024]{2,1,0:T(8,128)(2,1)}), bf16[2,1024,1024]{2,1,0:T(8,128)(2,1)}) %all-gather.11.cloned.1.call-update) | async-done | bytes 4194320 | tf_op jit(solution)/shard_map/all_gather | solution.py:139
  183.7 52.6 %all-gather.9.cloned.1.call-done = bf16[2,1024,1024]{2,1,0:T(8,128)(2,1)} async-done(((bf16[2,512,1024]{2,1,0:T(8,128)(2,1)}), bf16[2,1024,1024]{2,1,0:T(8,128)(2,1)}) %all-gather.9.cloned.1.call-update) | async-done | bytes 4194320 | tf_op jit(solution)/shard_map/all_gather | solution.py:140
  242.5 91.9 %while.26 = (s32[]{:T(128)}, bf16[2,1,512,16,64]{2,4,3,1,0:T(8,128)(2,1)}, f32[2,1,16,512]{3,2,1,0:T(8,128)S(1)}, bf16[2,1,1024,16,64]{2,4,3,1,0:T(8,128)(2,1)},...) while((s32[]{:T(128)}, ...), condition=%wide.region_5.6_spmd, body=%wide.region_2.5_spmd.sunk | while | flops 2223497216 | bytes 140773552 | solution.py:162
  242.5 15.2 %multiply_reduce_fusion.14 = (f32[16,512]{1,0:T(8,128)S(1)}, f32[16,512,1024]{2,1,0:T(8,128)}) fusion(bf16[2,1,1024,16,64]{2,4,3,1,0:T(8,128)(2,1)} %get-tuple-element.325, s32[]{:T(128)S(6)} %copy.240, bf16[2,1,512,16,64]{2,4,3,1,0:T(8,128)(2,1)S(1)} %get-tuple-element.324), kind=kOutput, calls=%fused_computation.2.clone.1 | convolution fusion | flops 1090510848 | bytes 36733952 | tf_op jit(solution)/shard_map/while/body/eval_jaxpr/gqhe,gkhe->ghqk/dot_general | solution.py:150
  257.6 16.2 %fusion.203 = f32[16,512]{1,0:T(8,128)S(1)} fusion(f32[16,512,1024]{2,1,0:T(8,128)} %get-tuple-element.293, f32[16,512]{1,0:T(8,128)S(1)} %get-tuple-element.294), kind=kLoop, calls=%fused_computation.3.clone.1 | loop fusion | flops 25157632 | bytes 33619968 | tf_op jit(solution)/shard_map/while/body/eval_jaxpr/reduce_sum | solution.py:155
  288.7 15.1 %multiply_reduce_fusion.14 = (f32[16,512]{1,0:T(8,128)S(1)}, f32[16,512,1024]{2,1,0:T(8,128)}) fusion(bf16[2,1,1024,16,64]{2,4,3,1,0:T(8,128)(2,1)} %get-tuple-element.325, s32[]{:T(128)S(6)} %copy.240, bf16[2,1,512,16,64]{2,4,3,1,0:T(8,128)(2,1)S(1)} %get-tuple-element.324), kind=kOutput, calls=%fused_computation.2.clone.1 | convolution fusion | flops 1090510848 | bytes 36733952 | tf_op jit(solution)/shard_map/while/body/eval_jaxpr/gqhe,gkhe->ghqk/dot_general | solution.py:150
  303.8 15.4 %fusion.203 = f32[16,512]{1,0:T(8,128)S(1)} fusion(f32[16,512,1024]{2,1,0:T(8,128)} %get-tuple-element.293, f32[16,512]{1,0:T(8,128)S(1)} %get-tuple-element.294), kind=kLoop, calls=%fused_computation.3.clone.1 | loop fusion | flops 25157632 | bytes 33619968 | tf_op jit(solution)/shard_map/while/body/eval_jaxpr/reduce_sum | solution.py:155
  346.6 16.0 %fusion.73 = f32[2,512,4096]{2,1,0:T(8,128)} fusion(bf16[2,512,1024]{2,1,0:T(8,128)(2,1)} %copy-done.11, bf16[1024,4096]{1,0:T(8,128)(2,1)} %all-gather.15.cloned.1.call-done), kind=kOutput, calls=%fused_computation.92 | convolution fusion | flops 8589934592 | bytes 27262976 | tf_op jit(solution)/shard_map/nlc,cd->nld/dot_general | solution.py:22
  375.7 39.2 %multiply_convert_fusion.3 = (bf16[2,512,4096]{2,1,0:T(8,128)(2,1)S(1)}, f32[2,512,4096]{2,1,0:T(8,128)}) fusion(f32[2,512,4096]{2,1,0:T(8,128)} %get-tuple-element.201, u8[512,4096]{1,0:T(8,128)(4,1)S(1)} %get-tuple-element.200), kind=kLoop, calls=%fused_computation.70 | loop fusion | flops 285212672 | bytes 44040192 | tf_op jit(solution)/shard_map/convert_element_type | solution.py:174
  420.3 21.2 %fusion.59 = bf16[2,512,4096]{2,1,0:T(8,128)(2,1)} fusion(f32[2,512,4096]{2,1,0:T(8,128)} %get-tuple-element.188, f32[2,512,4096]{2,1,0:T(8,128)} %get-tuple-element.201, f32[2,512,4096]{2,1,0:T(8,128)} %fusion.67, bf16[2,512,16]{1,2,0:T(8,128)(2,1)S(1)} %copy-done.44, bf16[2,4096,16]{1,0,2:T(2,128)(2,1)S(1)} %copy-done.29), kind=kOutput, calls=%fused_computation.64 | convolution fusion | flops 205520896 | bytes 59015168 | tf_op jit(solution)/shard_map/nlr,ncr->nlc/dot_general | solution.py:34
  478.3 261.5 %while.27 = (s32[]{:T(128)}, bf16[2,1,512,1024]{3,2,0,1:T(8,128)(2,1)}, bf16[2,1,512,1024]{3,2,0,1:T(8,128)(2,1)}, bf16[2,1,512,1024]{3,2,0,1:T(8,128)(2,1)}, bf...) while((s32[]{:T(128)}, ...), condition=%wide.region_14.15_spmd, body=%wide.region_10.14_spmd.sunk | while | flops 5473558528 | bytes 299075776 | solution.py:254
  478.5 14.8 %fusion.213 = f32[16,512,1024]{2,1,0:T(8,128)} fusion(bf16[2,1,1024,16,64]{2,4,3,1,0:T(8,128)(2,1)} %get-tuple-element.351, s32[]{:T(128)S(6)} %copy.250, bf16[2,1,512,16,64]{2,4,3,1,0:T(8,128)(2,1)S(1)} %get-tuple-element.352), kind=kOutput, calls=%fused_computation.31.clone.1 | convolution fusion | flops 1073741824 | bytes 36701184 | tf_op jit(solution)/shard_map/while/body/eval_jaxpr/gqhe,gkhe->ghqk/dot_general | solution.py:215
  493.3 15.5 %fusion.214 = bf16[16,64,1024]{2,1,0:T(8,128)(2,1)} fusion(f32[16,512,1024]{2,1,0:T(8,128)} %fusion.213, f32[16,512]{1,0:T(8,128)S(1)} %dynamic-slice_bitcast_fusion.2, bf16[2,1,512,16,64]{2,4,3,1,0:T(8,128)(2,1)} %get-tuple-element.354, s32[]{:T(128)S(6)} %copy.250), kind=kOutput, calls=%fused_computation.35.clone.1 | convolution fusion | flops 1099956224 | bytes 36732932 | tf_op jit(solution)/shard_map/while/body/eval_jaxpr/ghqk,gqhe->gkhe/dot_general | solution.py:220
  508.9 24.3 %multiply_reduce_fusion.15 = (f32[16,512]{1,0:T(8,128)S(1)}, f32[16,512,1024]{2,1,0:T(8,128)}) fusion(f32[16,512,1024]{2,1,0:T(8,128)} %fusion.213, f32[16,512]{1,0:T(8,128)S(1)} %dynamic-slice_bitcast_fusion.2, bf16[2,1,1024,16,64]{2,4,3,1,0:T(8,128)(2,1)} %get-tuple-element.355, s32[]{:T(128)S(6)} %copy.250, ...), kind=kOutput, calls=%fused_computation.20.clone.1 | convolution fusion | flops 1107288064 | bytes 70321152 | tf_op jit(solution)/shard_map/while/body/eval_jaxpr/gqhe,gkhe->ghqk/dot_general | solution.py:223
  533.2 28.1 %multiply_convert_fusion.13 = bf16[16,512,1024]{2,1,0:T(8,128)(2,1)} fusion(f32[16,512,1024]{2,1,0:T(8,128)} %get-tuple-element.304, f32[16,512,1024]{2,1,0:T(8,128)} %fusion.213, f32[16,512]{1,0:T(8,128)S(1)} %get-tuple-element.305, f32[16,512]{1,0:T(8,128)S(1)} %dynamic-slice_bitcast_fusion.2), kind=kLoop, calls=%fused_computation.19.clone.1 | loop fusion | flops 41943040 | bytes 83951616 | tf_op jit(solution)/shard_map/while/body/eval_jaxpr/convert_element_type | solution.py:227
  588.2 15.4 %reduce-scatter.3.cloned.1.call-done = bf16[1,512,1024]{1,2,0:T(8,128)(2,1)} async-done(((bf16[1,1024,1024]{1,2,0:T(8,128)(2,1)}), bf16[1,512,1024]{1,2,0:T(8,128)(2,1)}) %reduce-scatter.3.cloned.1.call-update) | async-done | bytes 1048592 | tf_op jit(solution)/shard_map/while/body/eval_jaxpr/reduce_scatter | solution.py:241
  624.0 15.5 %fusion.214 = bf16[16,64,1024]{2,1,0:T(8,128)(2,1)} fusion(f32[16,512,1024]{2,1,0:T(8,128)} %fusion.213, f32[16,512]{1,0:T(8,128)S(1)} %dynamic-slice_bitcast_fusion.2, bf16[2,1,512,16,64]{2,4,3,1,0:T(8,128)(2,1)} %get-tuple-element.354, s32[]{:T(128)S(6)} %copy.250), kind=kOutput, calls=%fused_computation.35.clone.1 | convolution fusion | flops 1099956224 | bytes 36732932 | tf_op jit(solution)/shard_map/while/body/eval_jaxpr/ghqk,gqhe->gkhe/dot_general | solution.py:220
  639.6 24.3 %multiply_reduce_fusion.15 = (f32[16,512]{1,0:T(8,128)S(1)}, f32[16,512,1024]{2,1,0:T(8,128)}) fusion(f32[16,512,1024]{2,1,0:T(8,128)} %fusion.213, f32[16,512]{1,0:T(8,128)S(1)} %dynamic-slice_bitcast_fusion.2, bf16[2,1,1024,16,64]{2,4,3,1,0:T(8,128)(2,1)} %get-tuple-element.355, s32[]{:T(128)S(6)} %copy.250, ...), kind=kOutput, calls=%fused_computation.20.clone.1 | convolution fusion | flops 1107288064 | bytes 70321152 | tf_op jit(solution)/shard_map/while/body/eval_jaxpr/gqhe,gkhe->ghqk/dot_general | solution.py:223
  663.9 28.0 %multiply_convert_fusion.13 = bf16[16,512,1024]{2,1,0:T(8,128)(2,1)} fusion(f32[16,512,1024]{2,1,0:T(8,128)} %get-tuple-element.304, f32[16,512,1024]{2,1,0:T(8,128)} %fusion.213, f32[16,512]{1,0:T(8,128)S(1)} %get-tuple-element.305, f32[16,512]{1,0:T(8,128)S(1)} %dynamic-slice_bitcast_fusion.2), kind=kLoop, calls=%fused_computation.19.clone.1 | loop fusion | flops 41943040 | bytes 83951616 | tf_op jit(solution)/shard_map/while/body/eval_jaxpr/convert_element_type | solution.py:227
  719.1 14.9 %reduce-scatter.3.cloned.1.call-done = bf16[1,512,1024]{1,2,0:T(8,128)(2,1)} async-done(((bf16[1,1024,1024]{1,2,0:T(8,128)(2,1)}), bf16[1,512,1024]{1,2,0:T(8,128)(2,1)}) %reduce-scatter.3.cloned.1.call-update) | async-done | bytes 1048592 | tf_op jit(solution)/shard_map/while/body/eval_jaxpr/reduce_scatter | solution.py:241
  792.1 161.0 %all-reduce.3.cloned.1.call-done = (f32[8,1024,16]{1,2,0:T(8,128)}, f32[8,16,3072]{2,1,0:T(8,128)}, f32[8,1024,16]{1,2,0:T(8,128)}, f32[8,16,1024]{2,1,0:T(8,128...) async-done(((f32[8,1024,16]{1,2,0:T(8,128)}, f32[8,16,3072]{2,1,0:T(8,128)}, f32[8,1024,16]{1,2,0:T(8,128)}, ...) | async-done | bytes 8388624 | tf_op jit(solution)/shard_map/psum | solution.py:273
  (310 shorter events, 290.0 us)
Async XLA Ops:
  7.2 51.5 %all-gather.7.cloned.1.call-start = ((), (), s32[]{:S(2)}) async-start(), calls=%async_computation.2 | async-start | bytes 7864320 | tf_op jit(solution)/shard_map/all_gather | solution.py:111
  7.9 110.7 %all-gather.17.cloned.1.call-start = ((), (), s32[]{:S(2)}) async-start(), calls=%async_computation.7 | async-start | bytes 10485760 | tf_op jit(solution)/shard_map/all_gather | solution.py:114
  8.7 168.8 %all-gather.11.cloned.1.call-start = ((), (), s32[]{:S(2)}) async-start(), calls=%async_computation.4 | async-start | bytes 6291456 | tf_op jit(solution)/shard_map/all_gather | solution.py:139
  11.8 47.0 %copy-start.51 = (f32[2,512]{1,0:T(2,128)}, f32[2,512]{1,0:T(2,128)S(1)}, u32[]{:S(2)}) copy-start(f32[2,512]{1,0:T(2,128)S(1)} %broadcast_multiply_fusion.1) | copy-start | bytes 12292
  13.1 54.6 %copy-start.57 = (f32[2,512]{1,0:T(2,128)}, f32[2,512]{1,0:T(2,128)S(1)}, u32[]{:S(2)}) copy-start(f32[2,512]{1,0:T(2,128)S(1)} %fusion.129) | copy-start | bytes 12292
  14.1 53.7 %copy-start.30 = (bf16[2,16,3072]{2,0,1:T(2,128)(2,1)}, bf16[2,16,3072]{2,0,1:T(2,128)(2,1)S(1)}, u32[]{:S(2)}) copy-start(bf16[2,16,3072]{2,0,1:T(2,128)(2,1)S(1)} %convolution_convert_fusion.2) | copy-start | bytes 589828
  15.0 52.7 %copy-start.60 = (bf16[2,512,16]{1,2,0:T(8,128)(2,1)}, bf16[2,512,16]{1,2,0:T(8,128)(2,1)S(1)}, u32[]{:S(2)}) copy-start(bf16[2,512,16]{1,2,0:T(8,128)(2,1)S(1)} %convolution_convert_fusion.11) | copy-start | bytes 98308
  73.2 163.1 %all-gather.9.cloned.1.call-start = ((), (), s32[]{:S(2)}) async-start(), calls=%async_computation.3 | async-start | bytes 6291456 | tf_op jit(solution)/shard_map/all_gather | solution.py:140
  73.8 262.6 %all-gather.13.cloned.1.call-start = ((), (), s32[]{:S(2)}) async-start(), calls=%async_computation.5 | async-start | bytes 2621440 | tf_op jit(solution)/shard_map/all_gather | solution.py:112
  74.3 272.2 %all-gather.15.cloned.1.call-start = ((), (), s32[]{:S(2)}) async-start(), calls=%async_computation.6 | async-start | bytes 10485760 | tf_op jit(solution)/shard_map/all_gather | solution.py:113
  75.6 43.0 %copy-start.66 = (f32[2]{0:T(128)}, f32[2]{0:T(128)S(1)}, u32[]{:S(2)}) copy-start(f32[2]{0:T(128)S(1)} %convert_element_type.223) | copy-start | bytes 28
  242.4 91.9 %copy-start.32 = (bf16[2,1024,16]{1,0,2:T(2,128)(2,1)S(1)}, bf16[2,1024,16]{1,0,2:T(2,128)(2,1)}, u32[]{:S(2)}) copy-start(bf16[2,1024,16]{1,0,2:T(2,128)(2,1)} %convolution_convert_fusion.6) | copy-start | bytes 196612
  257.6 16.2 %copy-start.8 = (bf16[2,1,1024,16,64]{2,4,3,1,0:T(8,128)(2,1)S(1)}, bf16[2,1,1024,16,64]{2,4,3,1,0:T(8,128)(2,1)}, u32[]{:S(2)}) copy-start(bf16[2,1,1024,16,64]{2,4,3,1,0:T(8,128)(2,1)} %get-tuple-element.323) | copy-start | bytes 12582916 | tf_op jit(solution)/shard_map/while
  257.6 16.2 %copy-start.19 = (bf16[2,1,512,16,64]{2,4,3,1,0:T(8,128)(2,1)S(1)}, bf16[2,1,512,16,64]{2,4,3,1,0:T(8,128)(2,1)}, u32[]{:S(2)}) copy-start(bf16[2,1,512,16,64]{2,4,3,1,0:T(8,128)(2,1)} %get-tuple-element.314) | copy-start | bytes 6291460 | tf_op jit(solution)/shard_map/while
  303.8 15.4 %copy-start.19 = (bf16[2,1,512,16,64]{2,4,3,1,0:T(8,128)(2,1)S(1)}, bf16[2,1,512,16,64]{2,4,3,1,0:T(8,128)(2,1)}, u32[]{:S(2)}) copy-start(bf16[2,1,512,16,64]{2,4,3,1,0:T(8,128)(2,1)} %get-tuple-element.314) | copy-start | bytes 6291460 | tf_op jit(solution)/shard_map/while
  346.5 16.0 %copy-start.24 = (bf16[2,16,4096]{2,0,1:T(2,128)(2,1)S(1)}, bf16[2,16,4096]{2,0,1:T(2,128)(2,1)}, u32[]{:S(2)}) copy-start(bf16[2,16,4096]{2,0,1:T(2,128)(2,1)} %convolution_convert_fusion.1) | copy-start | bytes 786436
  346.5 16.0 %copy-start.50 = (f32[4096]{0:T(1024)S(1)}, f32[4096]{0:T(1024)}, u32[]{:S(2)}) copy-start(f32[4096]{0:T(1024)} %param.44) | copy-start | bytes 49156
  375.7 39.3 %copy-start.29 = (bf16[2,4096,16]{1,0,2:T(2,128)(2,1)S(1)}, bf16[2,4096,16]{1,0,2:T(2,128)(2,1)}, u32[]{:S(2)}) copy-start(bf16[2,4096,16]{1,0,2:T(2,128)(2,1)} %convolution_convert_fusion) | copy-start | bytes 786436
  478.3 261.6 %copy-start.31 = (bf16[2,16,3072]{2,0,1:T(2,128)(2,1)S(1)}, bf16[2,16,3072]{2,0,1:T(2,128)(2,1)}, u32[]{:S(2)}) copy-start(bf16[2,16,3072]{2,0,1:T(2,128)(2,1)} %copy-done.30) | copy-start | bytes 589828
  478.4 108.2 %reduce-scatter.5.cloned.1.call-start = ((), (), s32[]{:S(2)}) async-start(), calls=%async_computation.10 | async-start | bytes 3145728 | tf_op jit(solution)/shard_map/while/body/eval_jaxpr/reduce_scatter | solution.py:244
  508.9 94.7 %reduce-scatter.3.cloned.1.call-start = ((), (), s32[]{:S(2)}) async-start(), calls=%async_computation.9 | async-start | bytes 3145728 | tf_op jit(solution)/shard_map/while/body/eval_jaxpr/reduce_scatter | solution.py:241
  609.2 108.4 %reduce-scatter.5.cloned.1.call-start = ((), (), s32[]{:S(2)}) async-start(), calls=%async_computation.10 | async-start | bytes 3145728 | tf_op jit(solution)/shard_map/while/body/eval_jaxpr/reduce_scatter | solution.py:244
  639.6 94.5 %reduce-scatter.3.cloned.1.call-start = ((), (), s32[]{:S(2)}) async-start(), calls=%async_computation.9 | async-start | bytes 3145728 | tf_op jit(solution)/shard_map/while/body/eval_jaxpr/reduce_scatter | solution.py:241
  739.8 213.2 %all-reduce.3.cloned.1.call-start = ((), (), s32[]{:S(2)}) async-start(), calls=%async_computation.8 | async-start | bytes 16777216 | tf_op jit(solution)/shard_map/psum | solution.py:273
  (73 other events, 313.8 us)
Sparse Core Ops, SparseCore 0:
  9.6 49.0 all-gather.6
  60.3 58.2 all-gather.16
  120.7 56.7 all-gather.10
  179.5 56.7 all-gather.8
  237.7 22.5 all-gather.12
  261.7 58.2 all-gather.14
  509.0 32.0 reduce-scatter.4
  571.5 32.0 reduce-scatter.2
  639.7 31.8 reduce-scatter.4
  702.2 31.7 reduce-scatter.2
  771.5 181.5 all-reduce.2
where the time goes:
time: 978 us; the launch traced here: 971 us
  matrix products  378 us (39%)
  waiting for transfers between devices  362 us (37%)
  other arithmetic  149 us (15%)
  local copies, waits for them, and re-layouts  64.1 us (7%)
  between operations  15.2 us (2%)
    psum x1, waiting for transfers between devices, shards(): lax.psum((fold(enter_first_terms), fold(enter_second_terms), fold(leave_f...  161 us
    convert_element_type x2, other arithmetic, attend_backward(): grad_scores = (probs * (grad_prob - inner)).astype(jnp.bfloat16)  56.1 us
    all_gather x1, waiting for transfers between devices, shards(): lax.all_gather(value_rows, 'seq', axis=1, tiled=True)  52.6 us
    dot_general x2, matrix products, attend_backward(): jnp.einsum('gqhe,gkhe->ghqk', grad_part, value_part, preferred_element_ty...  48.6 us
    all_gather x1, waiting for transfers between devices, shards(): lax.all_gather(inproj_weight, 'fsdp', axis=0, tiled=True)  43.7 us
    all_gather x1, waiting for transfers between devices, shards(): lax.all_gather(key_rows, 'seq', axis=1, tiled=True)  42.8 us
    dot_general x4, matrix products, project(): jnp.einsum('nlc,cd->nld', activation, matrix, preferred_element_type=jnp....  42.5 us
    dot_general x4, matrix products, project_back(): jnp.einsum('nld,cd->nlc', gradient, matrix, preferred_element_type=jnp.fl...  41.8 us
  transfers between devices with their start and end apart: 11, of which 7 were waited for; matrix products, arithmetic and copies ran while one was open for 35% of the time, Pallas kernels for 0%

commit v1 on v0

v1 whole, which is shorter than its diff:
```python
import functools
import math

import jax
import jax.numpy as jnp
from jax import lax
from jax.experimental import pallas as pl
from jax.experimental.pallas import tpu as pltpu
from jax.sharding import PartitionSpec as P

HEAD_DIM = 64
LANES = 128
epsilon = 1e-06

low = jnp.bfloat16
wide = jnp.float32


def dot_nn(left, right):
    return lax.dot_general(left, right, (((1,), (0,)), ((), ())), preferred_element_type=wide)


def dot_nt(left, right):
    return lax.dot_general(left, right, (((1,), (1,)), ((), ())), preferred_element_type=wide)


def dot_tn(left, right):
    return lax.dot_general(left, right, (((0,), (0,)), ((), ())), preferred_element_type=wide)


def normal_rows(values):
    center = values - jnp.mean(values, axis=-1, keepdims=True)
    spread = jnp.mean(center * center, axis=-1, keepdims=True)
    inverse = lax.rsqrt(spread + epsilon)
    return center * inverse, inverse


def layer_norm(values, gain, shift):
    return normal_rows(values)[0] * gain + shift


def layer_norm_back(gradient, values, gain):
    unit, inverse = normal_rows(values)
    scaled = gradient * gain
    mean_one = jnp.mean(scaled, axis=-1, keepdims=True)
    mean_two = jnp.mean(scaled * unit, axis=-1, keepdims=True)
    return inverse * (scaled - mean_one - unit * mean_two)


def for_rows(length, tile, body, start=0):
    def step(index, carry):
        body(pl.ds(pl.multiple_of(start + index * tile, tile), tile))
        return carry

    lax.fori_loop(0, length // tile, step, 0)


def attend_pairs(planes, out_ref, rest_ref, lse_ref, tile, splits=4):
    length = planes[0][0].shape[0]
    lane = lax.broadcasted_iota(jnp.int32, (1, LANES), 1)
    is_first = lane < HEAD_DIM
    size = length // splits
    keys, values, units = [], [], []
    for pair, (_, k_ref, v_ref) in enumerate(planes):
        keys.append([k_ref[n * size : (n + 1) * size, :] for n in range(splits)])
        values.append([])
        for n in range(splits):
            value = v_ref[n * size : (n + 1) * size, :]
            one = jnp.ones_like(value)
            values[pair].append((jnp.where(is_first, value, one), jnp.where(is_first, one, value)))
        units += [(pair, start, head) for start in range(0, length, tile) for head in range(2)]
    scores, tops, expos, products = {}, {}, {}, {}

    def finish(pair, start):
        rows = pl.ds(start, tile)
        mixed = [products.pop((pair, start, head)) for head in range(2)]
        total = jnp.where(
            is_first, pltpu.roll(mixed[0], HEAD_DIM, 1), pltpu.roll(mixed[1], HEAD_DIM, 1)
        )
        attended = jnp.where(is_first, mixed[0], mixed[1]) / total
        rounded = attended.astype(low)
        out_ref[pair, rows, :] = rounded
        rest_ref[pair, rows, :] = (attended - rounded.astype(wide)).astype(low)
        top = jnp.where(is_first, tops.pop((pair, start, 0)), tops.pop((pair, start, 1)))
        lse_ref[pair, rows, :] = top + jnp.log(total)

    for turn in range(len(units) + 2):
        if turn < len(units):
            pair, start, head = units[turn]
            query = planes[pair][0][pl.ds(start, tile), :] * low(0.125)
            zero = jnp.zeros_like(query)
            query = jnp.where(is_first, query, zero) if head == 0 else jnp.where(is_first, zero, query)
            highest = None
        for n in range(splits):
            if turn < len(units):
                part = dot_nt(query, keys[pair][n])
                scores[turn, n] = part
                for i in range(0, size, LANES):
                    column = part[:, i : i + LANES]
                    highest = column if highest is None else jnp.maximum(highest, column)
            if 0 <= turn - 1 < len(units):
                expo = jnp.exp(scores.pop((turn - 1, n)) - tops[units[turn - 1]])
                expos[turn - 1, n] = expo.astype(low)
        if turn < len(units):
            tops[units[turn]] = jnp.max(highest, axis=-1, keepdims=True)
        if turn >= 2:
            unit = units[turn - 2]
            expo = jnp.concatenate([expos.pop((turn - 2, n)) for n in range(splits)], axis=1)
            value = jnp.concatenate([values[unit[0]][n][unit[2]] for n in range(splits)], axis=0)
            products[unit] = dot_nn(expo, value)
            if unit[2] == 1:
                finish(*unit[:2])


def front_kernel(set_ref, tokens_ref, cot_ref, w0_ref, w1_ref, w2_ref, w3_ref, gain_ref, shift_ref,
                 bias_ref, table_refs,
                 x_out, c_out, g0_ref, g1_ref, g2_ref, g4_ref, normed_out, joined_out, low_ref,
                 picked_refs, att_ref, rest_ref, lse_ref,
                 x_s, c_s, normed_s, weight_s, joined_s, ow_s, ew_s, far_s, table_s, send_sem, recv_sem,
                 local_sem, *, sizes, tile, per):
    step = pl.program_id(0)
    steps = pl.num_programs(0) - 1
    count = sizes["seq"]
    lines = sizes["fsdp"] // 2
    rep, line = lax.axis_index("rep"), lax.axis_index("fsdp")
    seq = lax.axis_index("seq")
    core = lax.rem(line, 2)
    row = lax.div(line, 2)
    half = lax.rem(rep, 2)
    sibling = {"fsdp": line + 1 - 2 * core}
    pair = {"rep": rep + 1 - 2 * half}
    part = tokens_ref.shape[1]
    chunks, _, chunk = weight_s.shape
    tiles = chunk // LANES
    sends, locals_ = [], []

    def remote(source, target, device):
        position = len(sends)
        sends.append(
            pltpu.make_async_remote_copy(
                src_ref=source,
                dst_ref=target,
                send_sem=send_sem.at[position],
                recv_sem=recv_sem.at[position],
                device_id=device,
                device_id_type=pl.DeviceIdType.MESH,
            )
        )
        return sends[-1]

    def local(source, target):
        position = len(locals_)
        locals_.append(pltpu.make_async_copy(source, target, local_sem.at[position]))
        return locals_[-1]

    across = []
    for shift in range(1, lines):
        across.append(
            (
                {"fsdp": lax.rem(row + shift, lines) * 2 + core},
                lax.rem(row + lines - shift, lines) * 2 + core,
            )
        )
    around = [{"seq": lax.rem(seq + shift, count)} for shift in range(1, count)]

    def columns_of(shard, whole, start, size, chunked):
        height = shard.shape[0] // 2

        def own(which):
            return shard.at[pl.ds(which * height, height), pl.ds(start, size)]

        def placed(which_line, which):
            at = pl.multiple_of(which_line * 2 * height + which * height, height)
            if chunked:
                return whole.at[start // size, pl.ds(at, height), :]
            return whole.at[pl.ds(at, height), :]

        return own, placed

    def travel(own, placed):
        first, along, over, over_late = [], [], [], []
        for target, origin in across:
            first.append(remote(own(half), placed(line, half), target))
            along.append(remote(placed(origin, half), placed(origin, half), pair))
            over.append(remote(placed(origin, half), placed(origin, half), sibling))
            over_late.append(remote(placed(origin, 1 - half), placed(origin, 1 - half), sibling))
        return first, along, over, over_late

    def begin(copies):
        for copy in copies:
            copy.start()

    def arrived(copies):
        for copy in copies:
            copy.wait_recv()

    early, early_own = [], []
    for j in range(chunks):
        early.append(travel(*columns_of(w0_ref, weight_s, j * chunk, chunk, True)))
        height = w0_ref.shape[0]
        source = w0_ref.at[:, pl.ds(j * chunk, chunk)]
        target = weight_s.at[j, pl.ds(pl.multiple_of(line * height, height), height), :]
        early_own.append((remote(source, target, sibling), local(source, target)))
    late = [travel(*columns_of(w1_ref, ow_s, 0, w1_ref.shape[1], False))]
    splits = ew_s.shape[0]
    size = ew_s.shape[2]
    for j in range(splits):
        late.append(travel(*columns_of(w2_ref, ew_s, j * size, size, True)))
    deep = w3_ref.shape[0] // 4
    source = w3_ref.at[pl.ds(pl.multiple_of(half * deep, deep), deep), :]
    shrink_far = [
        remote(source, far_s.at[i], target) for i, (target, _) in enumerate(across)
    ]
    far_store = local(far_s, g4_ref)
    height = w1_ref.shape[0]
    mine = pl.ds(pl.multiple_of(line * height, height), height)
    late_own = [(remote(w1_ref, ow_s.at[mine, :], sibling), local(w1_ref, ow_s.at[mine, :]))]
    late_store = [local(ow_s, g1_ref)]
    for j in range(splits):
        source, target = w2_ref.at[:, pl.ds(j * size, size)], ew_s.at[j, mine, :]
        late_own.append((remote(source, target, sibling), local(source, target)))
        late_store.append(local(ew_s.at[j], g2_ref.at[j]))
    group = [0] + [1 + splits * i // 4 for i in range(1, 5)]

    def pass_on(pieces):
        for piece in pieces:
            arrived(piece[0])
            begin(piece[1])
            begin(piece[2])

    def pass_over(pieces):
        for piece in pieces:
            arrived(piece[1])
            begin(piece[3])

    def exchange(source, target):
        moves = []
        for shift, device in enumerate(around, 1):
            moves.append(
                remote(source.at[device["seq"]], target.at[pl.ds(shift * part, part), :], device)
            )
        return moves, local(source.at[seq], target.at[pl.ds(0, part), :])

    x_moves, x_own = exchange(tokens_ref, x_s)
    c_moves = [
        remote(cot_ref.at[device["seq"]], c_s.at[pl.ds((shift - 1) * part, part), :], device)
        for shift, device in enumerate(around, 1)
    ]
    c_store = local(c_s, c_out)
    table_loads = [local(table, held) for table, held in zip(table_refs, table_s)]
    x_store = local(x_s, x_out)
    normed_store = local(normed_s, normed_out)
    weight_store = local(weight_s, g0_ref)
    joined_store = local(joined_s, joined_out)

    assert (len(sends), len(locals_)) == (send_sem.shape[0], local_sem.shape[0])

    def take_tables(start, stop):
        which = set_ref[seq]
        for load, held, picked in zip(
            table_loads[start:stop], table_s[start:stop], picked_refs[start:stop]
        ):
            load.wait()
            picked[...] = held[which].astype(low)

    @pl.when(step == 0)
    def _():
        x_own.start()
        begin(table_loads[:2])
        barrier = pltpu.get_barrier_semaphore()
        peers = [sibling, pair, *around, *(target for target, _ in across)]
        for peer in peers:
            pl.semaphore_signal(barrier, inc=1, device_id=peer, device_id_type=pl.DeviceIdType.MESH)
        pl.semaphore_wait(barrier, len(peers))
        begin(early[0][0])
        begin(early[1][0])
        begin(x_moves)
        for j in range(chunks):
            early_own[j][0].start()
            early_own[j][1].start()
        take_tables(0, 2)
        first_ref, second_ref = picked_refs[:2]
        first = first_ref[...]

        def norm(start):
            def run(rows):
                normed = layer_norm(x_s[rows, :].astype(wide), gain_ref[...], shift_ref[...])
                normed = normed.astype(low)
                normed_s[rows, :] = normed
                low_ref[rows, :] = dot_nt(normed, first).astype(low)

            for_rows(part, tile, run, start)

        def project(j, start, length):
            columns = slice(j * chunk, (j + 1) * chunk)
            plane = j * chunk // x_s.shape[1]
            shift = max(plane - 1, 0) * x_s.shape[1]
            second = second_ref[:, columns]

            def run(rows):
                joined = dot_nn(normed_s[rows, :], weight_s[j])
                if plane != 1:
                    joined += bias_ref[:, columns.start - shift : columns.stop - shift]
                joined = (joined + 2.0 * dot_nn(low_ref[rows, :], second)).astype(low)
                for i in range(tiles):
                    joined_s[j * tiles + i, rows, :] = joined[:, i * LANES : (i + 1) * LANES]

            for_rows(length, tile, run, start)

        x_own.wait()
        norm(0)
        for turn in range(chunks + 2):
            if turn < chunks:
                arrived(early[turn][0])
                begin(early[turn][1])
                begin(early[turn][2])
                if turn + 2 < chunks:
                    begin(early[turn + 2][0])
                else:
                    begin(late[turn + 2 - chunks][0])
            if 0 <= turn - 1 < chunks:
                arrived(early[turn - 1][1])
                begin(early[turn - 1][3])
            if turn >= 2:
                j = turn - 2
                early_own[j][1].wait()
                arrived([early_own[j][0]])
                arrived(early[j][2])
                arrived(early[j][3])
                project(j, 0, part)
        for piece in late[2:]:
            begin(piece[0])
        begin(shrink_far)
        begin(table_loads[2:])
        for over, own in late_own:
            over.start()
            own.start()
        weight_store.start()
        for shift, move in enumerate(x_moves, 1):
            move.wait_recv()
            norm(shift * part)
        x_store.start()
        normed_store.start()
        for j in range(chunks):
            project(j, part, part * (count - 1))
        joined_store.start()
        pass_on(late[: group[1]])
        begin(c_moves)

    @pl.when(step == 2)
    def _():
        pass_on(late[group[1] : group[2]])

    @pl.when(step == 3)
    def _():
        pass_on(late[group[2] : group[3]])
        pass_over(late[: group[1]])

    @pl.when(step == 4)
    def _():
        pass_on(late[group[3] :])
        pass_over(late[group[1] : group[2]])

    @pl.when(step > 0)
    def _():
        pairs = joined_s.shape[0] // 3
        at = [(step - 1) * per + i for i in range(per)]
        attend_pairs(
            [
                (joined_s.at[i], joined_s.at[i + pairs], joined_s.at[i + 2 * pairs])
                for i in at
            ],
            att_ref,
            rest_ref,
            lse_ref,
            min(joined_s.shape[1], tile),
        )

    @pl.when(step == steps)
    def _():
        take_tables(2, len(table_loads))
        arrived(c_moves)
        c_store.start()
        arrived(shrink_far)
        far_store.start()
        pass_over(late[group[2] :])
        for over, own in late_own:
            over.wait_recv()
            own.wait()
        for piece, store in zip(late, late_store):
            arrived(piece[2])
            arrived(piece[3])
            store.start()
        for store in (*late_store, c_store, far_store):
            store.wait()
        for store in (x_store, normed_store, weight_store, joined_store):
            store.wait()
        for copy in sends:
            copy.wait_send()


def front(sizes, sets, tokens, cotangent, gain, shift, bias, weights, tables, tile=256):
    count, part, width = tokens.shape
    length = count * part
    rank, columns = tables[1].shape[1:]
    splits = 2 * sizes["fsdp"]
    expand = (splits, width, weights[2].shape[1] // splits)
    far = (length - part, width)
    pairs = width // LANES
    chunks = 6
    lines = sizes["fsdp"] // 2
    far_rows = (lines - 1, weights[3].shape[0] // 4, width)
    remotes = (lines - 1) * (4 * (chunks + 1 + splits) + 1) + chunks + 1 + splits + 2 * (count - 1)
    anywhere = pl.BlockSpec(memory_space=pl.ANY)
    once = pl.Buffered(1)

    def resident(shape):
        return pl.BlockSpec(shape, lambda i: (0,) * len(shape), pipeline_mode=once)

    per = 2
    planes = (pairs, length, LANES)
    block = pl.BlockSpec((per, length, LANES), lambda i: (jnp.maximum(i - 1, 0), 0, 0))
    image = jax.ShapeDtypeStruct((length, width), low)
    return pl.pallas_call(
        functools.partial(front_kernel, sizes=sizes, tile=min(tile, part), per=per),
        grid=(pairs // per + 1,),
        in_specs=[
            pl.BlockSpec(memory_space=pltpu.SMEM),
            *[anywhere] * 6,
            resident((1, width)),
            resident((1, width)),
            resident(bias.shape),
            [pl.BlockSpec(memory_space=pltpu.HBM)] * len(tables),
        ],
        out_specs=[
            *[anywhere] * 8,
            resident((length, rank)),
            [resident(table.shape[1:]) for table in tables],
            block,
            block,
            block,
        ],
        out_shape=[
            image,
            jax.ShapeDtypeStruct(far, low),
            jax.ShapeDtypeStruct((chunks, width, columns // chunks), low),
            jax.ShapeDtypeStruct((width, width), low),
            jax.ShapeDtypeStruct(expand, low),
            jax.ShapeDtypeStruct(far_rows, low),
            image,
            jax.ShapeDtypeStruct((columns // LANES, length, LANES), low),
            jax.ShapeDtypeStruct((length, rank), low),
            [jax.ShapeDtypeStruct(table.shape[1:], low) for table in tables],
            jax.ShapeDtypeStruct(planes, low),
            jax.ShapeDtypeStruct(planes, low),
            jax.ShapeDtypeStruct(planes, wide),
        ],
        scratch_shapes=[
            pltpu.VMEM((length, width), low),
            pltpu.VMEM(far, low),
            pltpu.VMEM((length, width), low),
            pltpu.VMEM((chunks, width, columns // chunks), low),
            pltpu.VMEM((columns // LANES, length, LANES), low),
            pltpu.VMEM((width, width), low),
            pltpu.VMEM(expand, low),
            pltpu.VMEM(far_rows, low),
            [pltpu.VMEM(table.shape, wide) for table in tables],
            pltpu.SemaphoreType.DMA((remotes,)),
            pltpu.SemaphoreType.DMA((remotes,)),
            pltpu.SemaphoreType.DMA((chunks + 9 + 2 * splits + len(tables),)),
        ],
        compiler_params=pltpu.CompilerParams(
            vmem_limit_bytes=61 << 20, collective_id=0, has_side_effects=True
        ),
        cost_estimate=pl.CostEstimate(
            flops=2 * length * width * columns + 16 * length * length * width,
            bytes_accessed=4 * width * (columns + 4 * length),
            transcendentals=length * length * width // HEAD_DIM,
        ),
        name="front",
    )(sets, tokens, cotangent, *weights, gain, shift, bias, list(tables))


def three_parts(values):
    high = values.astype(low)
    rest = values - high.astype(wide)
    middle = rest.astype(low)
    return high, middle, (rest - middle.astype(wide)).astype(low)


def attend_back_pair(q_ref, k_ref, v_ref, g_ref, o_ref, r_ref, lse_ref, out_ref, start, q_cols,
                     g_cols, key_sum, value_sum, tile, splits=4):
    columns = pl.ds(start, LANES)
    length = q_ref.shape[0]
    lane = lax.broadcasted_iota(jnp.int32, (1, LANES), 1)
    is_first = lane < HEAD_DIM
    size = length // splits
    q_cols[...] = jnp.transpose(q_ref[...] * low(0.125))
    g_cols[...] = jnp.transpose(g_ref[...])
    sides = {}
    for head in range(2):
        mine = is_first if head == 0 else ~is_first
        base = HEAD_DIM if head == 0 else 0
        ones = jnp.where((lane >= base) & (lane < base + 3), 1.0, 0.0).astype(low)
        for n in range(splits):
            key = k_ref[n * size : (n + 1) * size, :]
            value = v_ref[n * size : (n + 1) * size, :]
            sides[head, n] = (
                jnp.where(mine, key, ones),
                jnp.where(mine, value, ones),
                jnp.where(mine, key, jnp.zeros_like(key)),
            )

    def extend(head, rows_value, column):
        base = HEAD_DIM if head == 0 else 0
        high, middle, last = three_parts(column)
        pieces = jnp.where(
            lane == base,
            high,
            jnp.where(lane == base + 1, middle, jnp.where(lane == base + 2, last, low(0.0))),
        )
        return jnp.where(is_first if head == 0 else ~is_first, rows_value, pieces)

    def sides_of(begin, head):
        rows = pl.ds(begin, tile)
        grads = g_ref[rows, :]
        product = grads.astype(wide) * (o_ref[rows, :].astype(wide) + r_ref[rows, :].astype(wide))
        mine = is_first if head == 0 else ~is_first
        inner = jnp.sum(jnp.where(mine, product, 0.0), axis=-1, keepdims=True)
        logsum = lse_ref[rows, head * HEAD_DIM : head * HEAD_DIM + 1]
        return (
            extend(head, q_ref[rows, :] * low(0.125), -logsum),
            extend(head, grads, -inner),
        )

    units = [
        (begin, head, n)
        for begin in range(0, length, tile)
        for head in range(2)
        for n in range(splits)
    ]
    raw, made, query_grad = {}, {}, {}
    for turn in range(len(units) + 2):
        if turn < len(units):
            begin, head, n = units[turn]
            if n == 0:
                left = sides_of(begin, head)
            side = sides[head, n]
            raw[turn] = dot_nt(left[0], side[0]), dot_nt(left[1], side[1])
        if 0 <= turn - 1 < len(units):
            scores, change = raw.pop(turn - 1)
            probs = jnp.exp(scores)
            made[turn - 1] = probs.astype(low), (probs * change).astype(low)
        if turn >= 2:
            begin, head, n = units[turn - 2]
            prob_low, grad_scores = made.pop(turn - 2)
            span = slice(head * HEAD_DIM, (head + 1) * HEAD_DIM)
            rows = slice(begin, begin + tile)
            across = slice(n * size, (n + 1) * size)
            value_term = dot_nn(g_cols[span, rows], prob_low)
            key_term = dot_nn(q_cols[span, rows], grad_scores)
            if begin == 0:
                value_sum[span, across] = value_term
                key_sum[span, across] = key_term
            else:
                value_sum[span, across] += value_term
                key_sum[span, across] += key_term
            term = dot_nn(grad_scores, sides[head, n][2])
            query_grad[begin] = term if begin not in query_grad else query_grad[begin] + term
            if head == 1 and n == splits - 1:
                out_ref[0, rows, columns] = (query_grad.pop(begin) * 0.125).astype(low)
    out_ref[1, :, columns] = jnp.transpose(key_sum[...]).astype(low)
    out_ref[2, :, columns] = jnp.transpose(value_sum[...]).astype(low)


def join_planes(ref, rows):
    return jnp.concatenate([ref[i, rows, :] for i in range(ref.shape[0])], axis=1)


def feed_kernel(set_ref, live_ref, x_hbm, att_hbm, cot_ref, far_ref, obias_ref, oscale_ref, gain_ref,
                shift_ref, ebias_ref, sbias_ref, fscale_ref, ow_hbm, ew_ref, shard_ref, first_ref, o1_ref, o2_ref,
                e1_ref, e2_ref, s1_ref, s2_ref,
                result_out, gmid_out, gatt_out, terms_ref,
                x_ref, att_ref, ow_ref, middle_s, normed_s, gfeed_s, feed_s, gnormed_s, ew_s, sw_s, cot_s, result_ref, gmid_ref, gatt_ref, leave_s, widen_s,
                gnarrow_s, narrow_s, gwiden_s, to1_ref, to2_ref,
                te1_ref, te2_ref, ts1_ref, ts2_ref, send_sem, recv_sem, local_sem, out_sem, in_sem, *, sizes, tile,
                group):
    step = pl.program_id(0)
    steps = sizes["fsdp"]
    lines = steps // 2
    line, seq = lax.axis_index("fsdp"), lax.axis_index("seq")
    core = lax.rem(line, 2)
    row = lax.div(line, 2)
    sibling = {"fsdp": line + 1 - 2 * core}
    length, width = x_ref.shape
    tiles = width // LANES
    chunk = shard_ref.shape[0]
    block = chunk // 2
    live = live_ref[seq].astype(wide)
    sends, locals_ = [], []

    def remote(source, target, device):
        position = len(sends)
        sends.append(
            pltpu.make_async_remote_copy(
                src_ref=source,
                dst_ref=target,
                send_sem=send_sem.at[position],
                recv_sem=recv_sem.at[position],
                device_id=device,
                device_id_type=pl.DeviceIdType.MESH,
            )
        )
        return sends[-1]

    def local(source, target):
        position = len(locals_)
        locals_.append(pltpu.make_async_copy(source, target, local_sem.at[position]))
        return locals_[-1]

    def blocks_of(index):
        away, half = lax.div(index, 2), lax.rem(index, 2)
        far = lax.div(away + lines - 1, lines)
        at = lax.rem(row + lines - away, lines) * 2
        chosen = (at + core + half * (1 - 2 * core)) * 2
        first = far * ((at + core) * 2 + half) + (1 - far) * chosen
        second = far * ((at + 1 - core) * 2 + half) + (1 - far) * (chosen + 1)
        return first, second

    own = local(shard_ref, sw_s.at[0])
    own_over = remote(shard_ref, sw_s.at[1], sibling)
    rep = lax.axis_index("rep")
    side = lax.rem(rep, 2)
    pair = {"rep": rep + 1 - 2 * side}
    deep = block // 2
    far_moves, pair_moves, over_moves = [None, None], [None, None], [None, None]
    for away in range(1, lines):
        target = {"fsdp": lax.rem(row + away, lines) * 2 + core}
        for half in range(2):
            slot = 2 * away + half

            def here(which, over):
                at = pl.multiple_of(over * block + which * deep, deep)
                return sw_s.at[slot, pl.ds(at, deep), :]

            if half == 0:
                held = first_ref.at[away - 1]
                far_moves.append(local(held, here(side, 0)))
            else:
                held = here(side, 0)
                start = pl.multiple_of(block + side * deep, deep)
                far_moves.append(remote(shard_ref.at[pl.ds(start, deep), :], held, target))
            pair_moves.append(remote(held, here(side, 0), pair))
            over_moves.append(
                [
                    remote(held, here(side, 1), sibling),
                    remote(here(1 - side, 0), here(1 - side, 1), sibling),
                ]
            )
    ew_moves = []
    for index in range(steps):
        for i, which in enumerate(blocks_of(jnp.int32(index))):
            ew_moves.append(local(ew_ref.at[which], ew_s.at[2 * index + i]))

    near = cot_ref.shape[1]
    ow_move = local(ow_hbm, ow_ref)

    def incoming(i):
        rows = pl.ds(pl.multiple_of(i * tile, tile), tile)
        pairs = ((x_hbm.at[rows, :], x_ref.at[rows, :]), (att_hbm.at[:, rows, :], att_ref.at[:, rows, :]))
        return [
            pltpu.make_async_copy(source, target, in_sem.at[2 * i + k])
            for k, (source, target) in enumerate(pairs)
        ]

    cot_moves = [
        local(cot_ref.at[seq], cot_s.at[pl.ds(0, near), :]),
        local(far_ref, cot_s.at[pl.ds(near, length - near), :]),
    ]

    assert (len(sends), len(locals_)) == (send_sem.shape[0], local_sem.shape[0])

    def put(start, values):
        for i in range(values.shape[1] // LANES):
            at = start + i
            if group:
                at = at // group * (group + 1) + at % group
            terms_ref[at] = values[:, i * LANES : (i + 1) * LANES].astype(low)

    @pl.when(step == 0)
    def _():
        ow_move.start()
        for move in incoming(0):
            move.start()
        for move in cot_moves:
            move.start()
        for i in range(1, length // tile):
            for move in incoming(i):
                move.start()
        for move in (ew_moves[0], ew_moves[1], own):
            move.start()
        barrier = pltpu.get_barrier_semaphore()
        peers = [sibling, pair] + [
            {"fsdp": lax.rem(row + away, lines) * 2 + core} for away in range(1, lines)
        ]
        for peer in peers:
            pl.semaphore_signal(barrier, inc=1, device_id=peer, device_id_type=pl.DeviceIdType.MESH)
        pl.semaphore_wait(barrier, len(peers))
        for away in range(1, lines):
            far_moves[2 * away + 1].start()
            pair_moves[2 * away].start()
            over_moves[2 * away][0].start()
        own_over.start()

        def enter(rows):
            attended = join_planes(att_ref, rows)
            leave_low = dot_nt(attended, o1_ref[...]).astype(low)
            leave_s[rows, :] = leave_low
            branch = (
                dot_nn(attended, ow_ref[...])
                + obias_ref[...]
                + 2.0 * dot_nn(leave_low, o2_ref[...])
            )
            middle = x_ref[rows, :].astype(wide) + oscale_ref[...] * branch
            middle_s[rows, :] = middle
            normed = layer_norm(middle, gain_ref[...], shift_ref[...]).astype(low)
            normed_s[rows, :] = normed
            widen_s[rows, :] = dot_nt(normed, e1_ref[...]).astype(low)
            gfeed = (cot_s[rows, :].astype(wide) * live * fscale_ref[...]).astype(low)
            gfeed_s[rows, :] = gfeed
            gnarrow_s[rows, :] = (2.0 * dot_nt(gfeed, s2_ref[...])).astype(low)
            feed_s[rows, :] = jnp.zeros((tile, width), wide)
            gnormed_s[rows, :] = jnp.zeros((tile, width), wide)

        ow_move.wait()
        for move in cot_moves:
            move.wait()

        def enter_tile(i, carry):
            for move in incoming(i):
                move.wait()
            enter(pl.ds(pl.multiple_of(i * tile, tile), tile))
            return carry

        lax.fori_loop(0, length // tile, enter_tile, 0)
        narrow_s[...] = jnp.zeros_like(narrow_s)
        gwiden_s[...] = jnp.zeros_like(gwiden_s)

    def pass_on():
        @pl.when(step == 1)
        def _():
            for away in range(1, lines):
                near, later = 2 * away, 2 * away + 1
                far_moves[later].wait_recv()
                pair_moves[later].start()
                over_moves[later][0].start()
                pair_moves[near].wait_recv()
                over_moves[near][1].start()

        @pl.when(step == 2)
        def _():
            for away in range(1, lines):
                later = 2 * away + 1
                pair_moves[later].wait_recv()
                over_moves[later][1].start()

    for index in range(steps):
        @pl.when(step == index + 1)
        def _(index=index):
            ew_moves[2 * index].wait()
            ew_moves[2 * index + 1].wait()
            if index + 1 < steps:
                ew_moves[2 * index + 2].start()
                ew_moves[2 * index + 3].start()
                if index % 2:
                    far_moves[index + 1].start()
            if index == 0:
                own.wait()
            elif index == 1:
                own_over.wait_recv()
            else:
                if index % 2 == 0:
                    far_moves[index].wait()
                for move in over_moves[index]:
                    move.wait_recv()

    @pl.when((step > 0) & (step <= steps))
    def _():
        index = step - 1
        first, second = blocks_of(index)

        def part_of(table_ref):
            return jnp.concatenate(
                [
                    table_ref[:, pl.ds(pl.multiple_of(which * block, block), block)]
                    for which in (first, second)
                ],
                axis=1,
            )

        e2, s1, ebias = part_of(e2_ref), part_of(s1_ref), part_of(ebias_ref)
        inner, outer = chunk // 4, width // 4
        ts1_ref[...] = jnp.zeros_like(ts1_ref)
        te2_ref[...] = jnp.zeros_like(te2_ref)

        long_tile = 2 * tile

        def run(rows):
            normed, gfeed = normed_s[rows, :], gfeed_s[rows, :]
            widen_low, gnarrow = widen_s[rows, :], gnarrow_s[rows, :]
            widen_twice = widen_low * low(2.0)
            raw, made = [], []
            for n in range(5):
                if n < 4:
                    here = slice(n * inner, (n + 1) * inner)
                    held = slice(n % 2 * inner, (n % 2 + 1) * inner)
                    before = (
                        dot_nn(normed, ew_s[2 * index + n // 2, :, held])
                        + ebias[:, here]
                        + dot_nn(widen_twice, e2[:, here])
                    )
                    ghidden = dot_nt(gfeed, sw_s[index, here, :]) + dot_nn(gnarrow, s1[:, here])
                    raw.append((before, ghidden))
                if n:
                    before, ghidden = raw[n - 1]
                    ghidden = ghidden.astype(low).astype(wide)
                    scaled = before * math.sqrt(0.5)
                    share = 0.5 + 0.5 * lax.erf(scaled)
                    density = math.sqrt(0.5 / math.pi) * jnp.exp(-(scaled * scaled))
                    made.append(
                        (
                            (before * share).astype(low),
                            (ghidden * (share + before * density)).astype(low),
                        )
                    )
            hidden = jnp.concatenate([one[0] for one in made], axis=1)
            gbefore = jnp.concatenate([one[1] for one in made], axis=1)
            for n in range(4):
                there = slice(n * outer, (n + 1) * outer)
                feed_s[rows, there] += dot_nn(hidden, sw_s[index, :, there])
                gnormed_s[rows, there] += dot_nt(
                    gbefore[:, :block], ew_s[2 * index, there, :]
                ) + dot_nt(gbefore[:, block:], ew_s[2 * index + 1, there, :])
            narrow_s[rows, :] += dot_nt(hidden, s1)
            gwiden_s[rows, :] += dot_nt(gbefore, e2)
            ts1_ref[...] += dot_tn(gnarrow, hidden)
            te2_ref[...] += 2.0 * dot_tn(widen_low, gbefore)

        turns = length // long_tile

        def turn(i, carry):
            @pl.when(i == turns // 2)
            def _():
                pass_on()

            run(pl.ds(pl.multiple_of(i * long_tile, long_tile), long_tile))
            return carry

        lax.fori_loop(0, turns, turn, 0)
        block_tiles = block // LANES
        for i, which in enumerate((first, second)):
            here = slice(i * block, (i + 1) * block)
            start = 3 * tiles + which * block_tiles
            put(start, te2_ref[:, here])
            put(start + 2 * steps * block_tiles, ts1_ref[:, here])

    @pl.when(step == steps + 1)
    def _():
        o1, o2, e1, s2 = o1_ref[...], o2_ref[...], e1_ref[...], s2_ref[...]
        to1_ref[...] = jnp.zeros_like(to1_ref)
        to2_ref[...] = jnp.zeros_like(to2_ref)
        te1_ref[...] = jnp.zeros_like(te1_ref)
        ts2_ref[...] = jnp.zeros_like(ts2_ref)

        def leave(rows):
            middle = middle_s[rows, :]
            narrow_low = narrow_s[rows, :].astype(low)
            feed = feed_s[rows, :] + sbias_ref[...] + 2.0 * dot_nn(narrow_low, s2)
            result_ref[rows, :] = (live * (middle + fscale_ref[...] * feed)).astype(low)
            ts2_ref[...] += 2.0 * dot_tn(narrow_low, gfeed_s[rows, :])
            gwiden = (2.0 * gwiden_s[rows, :]).astype(low)
            te1_ref[...] += dot_tn(gwiden, normed_s[rows, :])
            gnormed = gnormed_s[rows, :] + dot_nn(gwiden, e1)
            gmiddle = cot_s[rows, :].astype(wide) * live + layer_norm_back(
                gnormed, middle, gain_ref[...]
            )
            gmid_ref[rows, :] = gmiddle
            gbranch = (gmiddle * oscale_ref[...]).astype(low)
            to2_ref[...] += 2.0 * dot_tn(leave_s[rows, :], gbranch)
            gleave = (2.0 * dot_nt(gbranch, o2)).astype(low)
            to1_ref[...] += dot_tn(gleave, join_planes(att_ref, rows))
            gatt = (dot_nt(gbranch, ow_ref[...]) + dot_nn(gleave, o1)).astype(low)
            for i in range(tiles):
                gatt_ref[i, rows, :] = gatt[:, i * LANES : (i + 1) * LANES]

        def outgoing(i):
            rows = pl.ds(pl.multiple_of(i * tile, tile), tile)
            pairs = (
                (result_ref.at[rows, :], result_out.at[rows, :]),
                (gmid_ref.at[rows, :], gmid_out.at[rows, :]),
                (gatt_ref.at[:, rows, :], gatt_out.at[:, rows, :]),
            )
            return [
                pltpu.make_async_copy(source, target, out_sem.at[3 * i + k])
                for k, (source, target) in enumerate(pairs)
            ]

        def leave_tile(i, carry):
            leave(pl.ds(pl.multiple_of(i * tile, tile), tile))
            for copy in outgoing(i):
                copy.start()
            return carry

        lax.fori_loop(0, length // tile, leave_tile, 0)
        put(0, to1_ref[...])
        put(tiles, to2_ref[...])
        put(2 * tiles, te1_ref[...])
        put(3 * tiles + 4 * steps * (block // LANES), ts2_ref[...])
        if group:
            for i in range(terms_ref.shape[0] // (group + 1)):
                kind = jnp.full(terms_ref.shape[1:], set_ref[seq], jnp.int32).astype(wide)
                terms_ref[i * (group + 1) + group] = kind.astype(low)
        for i in range(length // tile):
            for copy in outgoing(i):
                copy.wait()
        for copy in sends:
            copy.wait_send()


def feed_forward(sizes, sets, lives, values, attended, cotangent, far, obias, oscale, gain, shift, ebias,
                 sbias, fscale, oweight, eweight, shrink, first, o1, o2, e1, e2, s1, s2, group, tile=256):
    length, width = values.shape
    rank, hidden = e2.shape
    steps = sizes["fsdp"]
    chunk = hidden // steps
    once = pl.Buffered(1)

    def resident(shape):
        return pl.BlockSpec(shape, lambda i: (0,) * len(shape), pipeline_mode=once)

    anywhere = pl.BlockSpec(memory_space=pl.ANY)
    scalars = pl.BlockSpec(memory_space=pltpu.SMEM)
    vector = resident((1, width))
    table, table_wide = resident((rank, width)), resident((rank, hidden))
    term_tiles = (4 * width + 2 * hidden) // LANES
    if group:
        term_tiles += term_tiles // group
    terms = (term_tiles, rank, LANES)
    flops = 2 * length * width * (4 * hidden + 2 * width)
    remotes = 1 + 7 * (steps - 2) // 2
    return pl.pallas_call(
        functools.partial(feed_kernel, sizes=sizes, tile=tile, group=group),
        grid=(steps + 2,),
        in_specs=[
            scalars,
            scalars,
            anywhere,
            anywhere,
            anywhere,
            anywhere,
            vector,
            vector,
            vector,
            vector,
            resident((1, hidden)),
            vector,
            vector,
            anywhere,
            anywhere,
            anywhere,
            anywhere,
            table,
            table,
            table,
            table_wide,
            table_wide,
            table,
        ],
        out_specs=[anywhere, anywhere, anywhere, resident(terms)],
        scratch_shapes=[
            pltpu.VMEM((length, width), low),
            pltpu.VMEM(attended.shape, low),
            pltpu.VMEM((width, width), low),
            pltpu.VMEM((length, width), wide),
            pltpu.VMEM((length, width), low),
            pltpu.VMEM((length, width), low),
            pltpu.VMEM((length, width), wide),
            pltpu.VMEM((length, width), wide),
            pltpu.VMEM(eweight.shape, low),
            pltpu.VMEM((steps, chunk, width), low),
            pltpu.VMEM((length, width), low),
            pltpu.VMEM((length, width), low),
            pltpu.VMEM((length, width), wide),
            pltpu.VMEM(attended.shape, low),
            pltpu.VMEM((length, rank), low),
            pltpu.VMEM((length, rank), low),
            pltpu.VMEM((length, rank), low),
            pltpu.VMEM((length, rank), wide),
            pltpu.VMEM((length, rank), wide),
            pltpu.VMEM((rank, width), wide),
            pltpu.VMEM((rank, width), wide),
            pltpu.VMEM((rank, width), wide),
            pltpu.VMEM((rank, chunk), wide),
            pltpu.VMEM((rank, chunk), wide),
            pltpu.VMEM((rank, width), wide),
            pltpu.SemaphoreType.DMA((remotes,)),
            pltpu.SemaphoreType.DMA((remotes,)),
            pltpu.SemaphoreType.DMA((4 + 2 * steps + (steps - 2) // 2,)),
            pltpu.SemaphoreType.DMA((3 * (length // tile),)),
            pltpu.SemaphoreType.DMA((2 * (length // tile),)),
        ],
        out_shape=[
            jax.ShapeDtypeStruct((length, width), low),
            jax.ShapeDtypeStruct((length, width), wide),
            jax.ShapeDtypeStruct(attended.shape, low),
            jax.ShapeDtypeStruct(terms, low),
        ],
        compiler_params=pltpu.CompilerParams(
            vmem_limit_bytes=62 << 20, collective_id=2, has_side_effects=True
        ),
        cost_estimate=pl.CostEstimate(
            flops=flops,
            bytes_accessed=2 * width * (2 * hidden + width) + 14 * length * width,
            transcendentals=2 * length * hidden,
        ),
        name="feed",
    )(sets, lives, values, attended, cotangent, far, obias, oscale, gain, shift, ebias, sbias, fscale,
      oweight, eweight, shrink, first, o1, o2, e1, e2, s1, s2)


def back_kernel(q_ref, k_ref, v_ref, g_ref, o_ref, r_ref, lse_ref, result_ref, early_ref,
                weight_ref, x_ref, gmid_ref, normed_ref, low_ref, gain_ref, first_ref, second_ref,
                out_ref, grad_ref, early_out, late_out,
                q_cols, g_cols, key_sum, value_sum, joined_s, weight_s, x_s, gmid_s, normed_s,
                result_s, home_s, genter_s, terms_s, early_in, late_in, early_sum, late_sum,
                send_sem, recv_sem, swap_send, swap_recv, local_sem, *, sizes, summing,
                tile):
    step = pl.program_id(0)
    steps = pl.num_programs(0) - 1
    count, reps, lines = sizes["seq"], sizes["rep"], sizes["fsdp"] // 2
    devices = count * reps * lines * 2
    rep, line = lax.axis_index("rep"), lax.axis_index("fsdp")
    seq = lax.axis_index("seq")
    core = lax.rem(line, 2)
    row = lax.div(line, 2)
    sets = early_sum.shape[0]
    part = out_ref.shape[1]
    sends, locals_ = [], []

    def place(core_at, seq_at, row_at, rep_at):
        return ((core_at * count + seq_at) * lines + row_at) * reps + rep_at

    mine = place(core, seq, row, rep)

    def remote(source, target, device):
        position = len(sends)
        sends.append(
            pltpu.make_async_remote_copy(
                src_ref=source,
                dst_ref=target,
                send_sem=send_sem.at[position],
                recv_sem=recv_sem.at[position],
                device_id=device,
                device_id_type=pl.DeviceIdType.MESH,
            )
        )
        return sends[-1]

    def local(source, target):
        position = len(locals_)
        locals_.append(pltpu.make_async_copy(source, target, local_sem.at[position]))
        return locals_[-1]

    def begin(copies):
        for copy in copies:
            copy.start()

    def arrived(copies):
        for copy in copies:
            copy.wait_recv()

    def other(offset):
        spot = lax.rem(mine + offset, devices)
        rep_at = lax.rem(spot, reps)
        row_at = lax.rem(lax.div(spot, reps), lines)
        seq_at = lax.rem(lax.div(spot, reps * lines), count)
        core_at = lax.div(spot, reps * lines * count)
        return spot, {"rep": rep_at, "fsdp": row_at * 2 + core_at, "seq": seq_at}

    def swap(phase, offset, source, target):
        spot, device = other(offset)
        size = source.shape[0] // devices
        return pltpu.make_async_remote_copy(
            src_ref=source.at[pl.ds(spot * size, size)],
            dst_ref=target.at[offset],
            send_sem=swap_send.at[phase, offset],
            recv_sem=swap_recv.at[phase, offset],
            device_id=device,
            device_id_type=pl.DeviceIdType.MESH,
        )

    def each_other(body):
        def turn(offset, carry):
            body(offset)
            return carry

        lax.fori_loop(1, devices, turn, 0)

    def add_by_set(source, kinds, target):
        for index in range(target.shape[1]):
            def turn(offset, totals):
                kind = kinds[offset, kinds.shape[1] - 1].astype(wide)
                piece = source[offset, index].astype(wide)
                return tuple(
                    total + jnp.where(kind == float(which), piece, 0.0)
                    for which, total in enumerate(totals)
                )

            zero = jnp.zeros(target.shape[2:], wide)
            totals = lax.fori_loop(0, devices, turn, (zero,) * sets)
            for which, total in enumerate(totals):
                target[which, index] = total.astype(low)

    def stages(piece, whole):
        along_rep = [{"rep": lax.rem(rep + s, reps)} for s in range(1, reps)]
        along_row = [{"fsdp": lax.rem(row + s, lines) * 2 + core} for s in range(1, lines)]
        along_seq = [{"seq": lax.rem(seq + s, count)} for s in range(1, count)]
        ones, others = pl.ds(0, sets // 2), pl.ds(sets // 2, sets // 2)
        every = pl.ds(0, sets)

        def send(start, size, which, targets):
            block = whole.at[pl.ds(start, size), which]
            return [remote(block, block, target) for target in targets]

        line_start = place(core, seq, row, 0)
        moves = [send(mine, 1, every, along_rep)]
        moves.append(
            send(line_start, reps, ones, along_row) + send(line_start, reps, others, along_seq)
        )
        last = send(place(core, seq, 0, 0), reps * lines, ones, along_seq)
        for s in range(count):
            last += send(place(core, s, row, 0), reps, others, along_row)
        moves.append(last)
        moves.append(
            send(place(core, 0, 0, 0), reps * lines * count, every, [{"fsdp": line + 1 - 2 * core}])
        )
        return local(piece, whole.at[mine]), moves

    def late_stages(piece, whole):
        every = pl.ds(0, sets)

        def send(start, size, targets):
            block = whole.at[pl.ds(start, size), every]
            return [remote(block, block, target) for target in targets]

        moves = [send(mine, 1, [{"seq": lax.rem(seq + s, count)} for s in range(1, count)]), [], []]
        for s in range(count):
            moves[1] += send(
                place(core, s, row, rep), 1, [{"rep": lax.rem(rep + i, reps)} for i in range(1, reps)]
            )
            moves[2] += send(
                place(core, s, row, 0),
                reps,
                [{"fsdp": lax.rem(row + i, lines) * 2 + core} for i in range(1, lines)],
            )
        moves.append(
            send(place(core, 0, 0, 0), reps * lines * count, [{"fsdp": line + 1 - 2 * core}])
        )
        return local(piece, whole.at[mine]), moves

    if summing:
        early_keep, early_moves = stages(early_sum, early_out)
        late_keep, late_moves = late_stages(late_sum, late_out)
    around = [lax.rem(seq + shift, count) for shift in range(1, count)]
    result_moves = [
        remote(result_s.at[pl.ds(shift * part, part), :], out_ref.at[seq], {"seq": to})
        for shift, to in enumerate(around, 1)
    ]
    result_load = local(result_ref, result_s)
    result_own = local(result_s.at[pl.ds(0, part), :], out_ref.at[seq])
    short = min(tile, part)
    grad_moves = [
        [
            [
                remote(
                    home_s.at[pl.ds(shift * part + start, short), :],
                    grad_ref.at[seq, pl.ds(start, short), :],
                    {"seq": to},
                )
            ]
            for start in range(0, part, short)
        ]
        for shift, to in enumerate(around, 1)
    ]
    grad_own = local(home_s.at[pl.ds(0, part), :], grad_ref.at[seq])
    loads = [
        local(weight_ref, weight_s),
        local(x_ref, x_s),
        local(gmid_ref, gmid_s),
        local(normed_ref, normed_s),
    ]
    keep_sem = local_sem.at[len(locals_)]

    assert len(sends) == send_sem.shape[0] and len(locals_) < local_sem.shape[0]

    @pl.when(step == 0)
    def _():
        result_load.start()
        barrier = pltpu.get_barrier_semaphore()

        def greet(device):
            pl.semaphore_signal(
                barrier, inc=1, device_id=device, device_id_type=pl.DeviceIdType.MESH
            )

        if summing:
            each_other(lambda offset: greet(other(offset)[1]))
            pl.semaphore_wait(barrier, devices - 1)
            size = early_ref.shape[0] // devices
            keep = pltpu.make_async_copy(
                early_ref.at[pl.ds(mine * size, size)], early_in.at[0], keep_sem
            )
            keep.start()
            each_other(lambda offset: swap(0, offset, early_ref, early_in).start())
            keep.wait()
        else:
            for to in around:
                greet({"seq": to})
            pl.semaphore_wait(barrier, count - 1)
        result_load.wait()
        begin(result_moves)
        result_own.start()

    if summing:
        @pl.when(step == 3)
        def _():
            each_other(lambda offset: swap(0, offset, early_ref, early_in).wait_recv())
            add_by_set(early_in, early_in, early_sum)
            early_keep.start()
            early_keep.wait()
            begin(early_moves[0])

        for number, at in ((1, 5), (2, 7)):
            @pl.when(step == at)
            def _(number=number):
                arrived(early_moves[number - 1])
                begin(early_moves[number])

    for number, load in enumerate(loads):
        @pl.when(step == number + 2)
        def _(load=load):
            load.start()

    @pl.when(step < steps)
    def _():
        attend_back_pair(
            q_ref.at[0], k_ref.at[0], v_ref.at[0], g_ref.at[0], o_ref.at[0], r_ref.at[0],
            lse_ref.at[0], joined_s,
            pl.multiple_of(step * LANES, LANES), q_cols, g_cols, key_sum, value_sum, tile,
        )

    @pl.when(step == steps)
    def _():
        first = first_ref[...]
        width = x_s.shape[1]
        planes = joined_s.shape[0]
        tiles = width // LANES
        length = x_s.shape[0]
        chunk = weight_s.shape[2]
        per = width // chunk
        seconds = [
            second_ref[:, p * width : (p + 1) * width] for p in range(planes)
        ]
        for load in loads:
            load.wait()

        def enter_back(rows):
            genter = dot_nt(joined_s[0, rows, :], seconds[0])
            for p in range(1, planes):
                genter += dot_nt(joined_s[p, rows, :], seconds[p])
            genter_s[rows, :] = (2.0 * genter).astype(low)

        for_rows(length, tile, enter_back)

        def leave(rows):
            gnormed = dot_nn(genter_s[rows, :], first)
            for p in range(planes):
                for i in range(per):
                    gnormed += dot_nt(
                        joined_s[p, rows, i * chunk : (i + 1) * chunk], weight_s[p * per + i]
                    )
            back = layer_norm_back(gnormed, x_s[rows, :].astype(wide), gain_ref[...])
            home_s[rows, :] = (gmid_s[rows, :] + back).astype(low)

        for p in range(planes + 1):
            if p == 0:
                values = dot_tn(genter_s[...], normed_s[...]).astype(low)
            else:
                values = (2.0 * dot_tn(low_ref[...], joined_s[p - 1])).astype(low)
            for i in range(tiles):
                terms_s[p * tiles + i] = values[:, i * LANES : (i + 1) * LANES]
        if summing:
            size = terms_s.shape[0] // devices
            keep = pltpu.make_async_copy(
                terms_s.at[pl.ds(mine * size, size)], late_in.at[0], keep_sem
            )
            keep.start()
            each_other(lambda offset: swap(1, offset, terms_s, late_in).start())
            keep.wait()
        else:
            keep = pltpu.make_async_copy(terms_s, late_out, keep_sem)
            keep.start()
            keep.wait()
        far_rows = list(range(part, length, short))

        def run_far():
            start = far_rows.pop(0)
            for_rows(short, short, leave, start)
            return grad_moves[start // part - 1][(start % part) // short]

        ready = run_far()
        if summing:
            each_other(lambda offset: swap(1, offset, terms_s, late_in).wait_recv())
            add_by_set(late_in, early_in, late_sum)
            late_keep.start()
            late_keep.wait()
            begin(late_moves[0])
        begin(ready)
        if summing:
            arrived(early_moves[2])
            begin(early_moves[3])
        while far_rows:
            begin(run_far())
        number = 1
        for start in range(0, part, short):
            if summing and number < 3:
                arrived(late_moves[number - 1])
                begin(late_moves[number])
                number += 1
            for_rows(short, short, leave, start)
        grad_own.start()
        if summing:
            while number < 4:
                arrived(late_moves[number - 1])
                begin(late_moves[number])
                number += 1
            arrived(late_moves[3])
            arrived(early_moves[3])
        arrived(result_moves)
        for moves in grad_moves:
            for pieces in moves:
                arrived(pieces)
        result_own.wait()
        grad_own.wait()
        for copy in sends:
            copy.wait_send()
        if summing:
            each_other(lambda offset: swap(0, offset, early_ref, early_in).wait_send())
            each_other(lambda offset: swap(1, offset, terms_s, late_in).wait_send())


def back(sizes, summing, set_count, joined, grads, attended, rest, logsum, result, early, weight,
         values, gmiddle, normed, enter_low, gain, first, second, tile=256):
    length, width = values.shape
    count = sizes["seq"]
    devices = count * sizes["rep"] * sizes["fsdp"]
    rank = enter_low.shape[1]
    pairs = width // LANES
    late_tiles = 4 * pairs
    if summing:
        early_size, late_size = early.shape[0] // devices, late_tiles // devices
        early_shape = (devices, set_count, early_size - 1, rank, LANES)
        late_shape = (devices, set_count, late_size, rank, LANES)
    else:
        early_size, late_size = 2, 1
        early_shape, late_shape = (1, rank, LANES), (late_tiles, rank, LANES)
    part = length // count
    once = pl.Buffered(1)
    anywhere = pl.BlockSpec(memory_space=pl.ANY)

    def resident(shape):
        return pl.BlockSpec(shape, lambda i: (0,) * len(shape), pipeline_mode=once)

    def plane(start):
        return pl.BlockSpec(
            (1, length, LANES), lambda i: (jnp.minimum(i, pairs - 1) + start, 0, 0)
        )

    lines = sizes["fsdp"] // 2
    spread = sizes["rep"] - 1 + (lines - 1) * (1 + count) + 2 * (count - 1) + 1
    late_spread = (count - 1) + count * (sizes["rep"] - 1 + lines - 1) + 1
    remotes = (spread + late_spread if summing else 0) + (count - 1) * (1 + part // min(tile, part))
    home = jax.ShapeDtypeStruct((count, part, width), low)
    return pl.pallas_call(
        functools.partial(back_kernel, sizes=sizes, summing=summing, tile=tile),
        grid=(pairs + 1,),
        in_specs=[
            plane(0),
            plane(pairs),
            plane(2 * pairs),
            plane(0),
            plane(0),
            plane(0),
            plane(0),
            anywhere,
            anywhere,
            anywhere,
            anywhere,
            anywhere,
            anywhere,
            resident((length, rank)),
            resident((1, width)),
            resident(first.shape),
            resident(second.shape),
        ],
        out_specs=[anywhere] * 4,
        out_shape=[
            home,
            home,
            jax.ShapeDtypeStruct(early_shape, low),
            jax.ShapeDtypeStruct(late_shape, low),
        ],
        scratch_shapes=[
            pltpu.VMEM((LANES, length), low),
            pltpu.VMEM((LANES, length), low),
            pltpu.VMEM((LANES, length), wide),
            pltpu.VMEM((LANES, length), wide),
            pltpu.VMEM((3, length, width), low),
            pltpu.VMEM(weight.shape, low),
            pltpu.VMEM((length, width), low),
            pltpu.VMEM((length, width), wide),
            pltpu.VMEM((length, width), low),
            pltpu.VMEM((length, width), low),
            pltpu.VMEM((length, width), low),
            pltpu.VMEM((length, rank), low),
            pltpu.VMEM((late_tiles, rank, LANES), low),
            pltpu.VMEM((devices, early_size, rank, LANES), low),
            pltpu.VMEM((devices, late_size, rank, LANES), low),
            pltpu.VMEM((set_count, early_size - 1, rank, LANES), low),
            pltpu.VMEM((set_count, late_size, rank, LANES), low),
            pltpu.SemaphoreType.DMA((remotes,)),
            pltpu.SemaphoreType.DMA((remotes,)),
            pltpu.SemaphoreType.DMA((2, devices)),
            pltpu.SemaphoreType.DMA((2, devices)),
            pltpu.SemaphoreType.DMA((10,)),
        ],
        compiler_params=pltpu.CompilerParams(
            vmem_limit_bytes=60 << 20, collective_id=1, has_side_effects=True
        ),
        cost_estimate=pl.CostEstimate(
            flops=40 * length * length * width + 6 * length * width * width,
            bytes_accessed=40 * length * width,
            transcendentals=length * length * width // HEAD_DIM,
        ),
        name="back",
    )(joined, joined, joined, grads, attended, rest, logsum, result, early, weight, values,
      gmiddle, normed, enter_low, gain, first, second)


def lay_out_kernel(images, sources, kept, targets, *, tiles):
    targets = list(targets)
    for image, out in zip(images, kept):
        out[...] = image[...]
    for source, widths in zip(sources, tiles):
        size = source.shape[2]
        position = 0
        for width in widths:
            target = targets.pop(0)
            for i in range(width):
                piece = source[position // size, :, position % size]
                target[:, :, i * LANES : (i + 1) * LANES] = piece.astype(wide)
                position += 1


def lay_out(images, sources, widths, together=2):
    set_count = sources[0].shape[1]
    rank = sources[0].shape[3]
    tiles = tuple(tuple(width // LANES for width in group) for group in widths)
    flat = [width for group in widths for width in group]
    steps = set_count // together
    count, part, size = images[0].shape
    image = pl.BlockSpec((count, part // steps, size), lambda i: (0, i, 0))
    return pl.pallas_call(
        functools.partial(lay_out_kernel, tiles=tiles),
        grid=(steps,),
        in_specs=[
            [image] * len(images),
            [
                pl.BlockSpec(
                    (source.shape[0], together, source.shape[2], rank, LANES),
                    lambda i: (0, i, 0, 0, 0),
                )
                for source in sources
            ],
        ],
        out_specs=[
            [image] * len(images),
            [pl.BlockSpec((together, rank, width), lambda i: (i, 0, 0)) for width in flat],
        ],
        out_shape=[
            [jax.ShapeDtypeStruct(one.shape, one.dtype) for one in images],
            [jax.ShapeDtypeStruct((set_count, rank, width), wide) for width in flat],
        ],
        compiler_params=pltpu.CompilerParams(vmem_limit_bytes=60 << 20),
        cost_estimate=pl.CostEstimate(
            flops=0, bytes_accessed=6 * set_count * rank * sum(flat), transcendentals=0
        ),
        name="lay_out",
    )(list(images), list(sources))


def sum_by_set(terms, choose, axes, devices):
    tiles, rank, _ = terms.shape
    sets = choose.shape[1]
    pieces = lax.all_to_all(terms.reshape(devices, -1), axes, 0, 0, tiled=True)
    summed = jnp.einsum("ns,nx->sx", choose, pieces, preferred_element_type=wide).astype(low)
    whole = lax.all_gather(summed, axes, axis=1, tiled=True)
    whole = whole.reshape(sets, tiles, rank, LANES)
    return whole.transpose(0, 2, 1, 3).reshape(sets, rank, tiles * LANES).astype(wide)


def shards(
    tokens,
    cotangent,
    adapter_set,
    image_live,
    first_gain,
    first_shift,
    inproj_weight,
    inproj_bias,
    outproj_weight,
    outproj_bias,
    attend_scale,
    second_gain,
    second_shift,
    expand_weight,
    expand_bias,
    shrink_weight,
    shrink_bias,
    feedfwd_scale,
    inproj_first,
    inproj_second,
    outproj_first,
    outproj_second,
    expand_first,
    expand_second,
    shrink_first,
    shrink_second,
    *,
    sizes,
):
    count = sizes["seq"]
    axes = ("rep", "fsdp", "seq")
    devices = sizes["rep"] * sizes["fsdp"] * count
    set_count = inproj_first.shape[0]
    def row(vector):
        return vector.reshape(1, vector.shape[0])

    def flip(table):
        return jnp.swapaxes(table, 1, 2)

    (
        values, far, whole_inproj, whole_outproj, whole_expand, far_shrink, normed,
        joined, enter_low, picked, attended, rest, logsum,
    ) = front(
        sizes, adapter_set, tokens, cotangent, row(first_gain), row(first_shift), row(inproj_bias),
        (inproj_weight, outproj_weight, expand_weight, shrink_weight),
        (
            flip(inproj_first), inproj_second, flip(outproj_first), outproj_second,
            flip(expand_first), expand_second, flip(shrink_first), shrink_second,
        ),
    )
    enter_first, enter_second, *feed_tables = picked
    late_tables = (inproj_first, inproj_second)
    early_tables = (
        outproj_first, outproj_second, expand_first, expand_second, shrink_first, shrink_second
    )
    rank = inproj_second.shape[1]
    widths = [
        [table.shape[1] * table.shape[2] // rank for table in tables]
        for tables in (late_tables, early_tables)
    ]
    tiles = [sum(group) // LANES for group in widths]
    summing = all(tile % devices == 0 for tile in tiles)
    result, gmiddle, gattended, early = feed_forward(
        sizes, adapter_set, image_live, values, attended, cotangent, far, row(outproj_bias),
        row(attend_scale), row(second_gain), row(second_shift), row(expand_bias), row(shrink_bias),
        row(feedfwd_scale), whole_outproj, whole_expand, shrink_weight, far_shrink, *feed_tables,
        tiles[1] // devices if summing else 0,
    )
    block_output, input_grad, early_sums, late_sums = back(
        sizes, summing, set_count, joined, gattended, attended, rest, logsum, result, early,
        whole_inproj, values, gmiddle, normed, enter_low, row(first_gain), enter_first,
        enter_second,
    )
    if summing:
        (block_output, input_grad), tables = lay_out(
            (block_output, input_grad), (late_sums, early_sums), widths
        )
    else:
        index = lax.dynamic_slice_in_dim(adapter_set, lax.axis_index("seq"), 1)
        sets = lax.all_gather(index, axes, axis=0, tiled=True)
        choose = (sets[:, None] == jnp.arange(set_count)[None, :]).astype(low)
        tables = []
        for terms, group in ((late_sums, widths[0]), (early, widths[1])):
            whole = sum_by_set(terms, choose, axes, devices)
            start = 0
            for size in group:
                tables.append(whole[:, :, start : start + size])
                start += size
    tables = [flip(table) if i % 2 == 0 else table for i, table in enumerate(tables)]
    return (block_output, input_grad, *tables)


def solution(mesh):
    images = P(("rep", "fsdp"), "seq", None)
    slots = P(("rep", "fsdp"))
    rows = P("fsdp", None)
    whole = P()
    return jax.shard_map(
        functools.partial(shards, sizes=dict(mesh.shape)),
        mesh=mesh,
        in_specs=(
            images, images, slots, slots, whole, whole, rows, whole, rows, whole, whole, whole,
            whole, rows, whole, rows, whole, whole, whole, whole, whole, whole, whole, whole, whole,
            whole,
        ),
        out_specs=(images, images) + (whole,) * 8,
        check_vma=False,
    )
```

time: 978 us -> 249 us (0.25)
  matrix products: 378 us -> 0 us
  waiting for transfers between devices: 362 us -> 0 us
  Pallas kernels: 0 us -> 247 us
  other arithmetic: 149 us -> 0 us
  local copies, waits for them, and re-layouts: 64.1 us -> 0 us
  between operations: 15.2 us -> 0.85 us
    dot_general x54 -> x0, matrix products: 378 us -> none  [the longest x2 48.6 us: attend_backward(): jnp.einsum('gqhe,gkhe->ghqk', grad_part, value_part, preferred_element_ty...]
    pallas_call x0 -> x4, Pallas kernels: none -> 247 us  [the longest x1 87.5 us: back(): pl.pallas_call(functools.partial(back_kernel, sizes=sizes, summing=summin...]
    all_gather x6 -> x0, waiting for transfers between devices: 168 us -> none  [the longest x1 52.6 us: shards(): lax.all_gather(value_rows, 'seq', axis=1, tiled=True)]
    psum x1 -> x0, waiting for transfers between devices: 161 us -> none  [shards(): lax.psum((fold(enter_first_terms), fold(enter_second_terms), fold(leave_f...]
    convert_element_type x16 -> x0, other arithmetic: 105 us -> none  [the longest x2 56.1 us: attend_backward(): grad_scores = (probs * (grad_prob - inner)).astype(jnp.bfloat16)]
    reduce_sum x12 -> x0, other arithmetic: 43.5 us -> none  [the longest x2 31.6 us: attend_forward(): total = jnp.sum(expo, axis=-1, keepdims=True)]
    reduce_scatter x4 -> x0, waiting for transfers between devices: 30.3 us -> none  [the longest x2 30.3 us: attend_backward(): lax.psum_scatter(key_term.astype(jnp.bfloat16), 'seq', scatter_dimension=...]
    dynamic_update_slice x12 -> x0, local copies, waits for them, and re-layouts: 21.4 us -> none  [shards(): lax.map(attend_backward, (query_blocks, key_blocks, value_blocks, grad_bl...]
  transfers between devices with their start and end apart: 11 -> 0, of which waited for: 7 -> 0; matrix products, arithmetic and copies ran while one was open for 35% -> 0% of each run, Pallas kernels for 0% -> 0%
where the time goes in v1:
time: 249 us; the launch traced here: 248 us
  Pallas kernels  247 us (99%)
    pallas_call x1, Pallas kernels, back(): pl.pallas_call(functools.partial(back_kernel, sizes=sizes, summing=summin...  87.5 us
    pallas_call x1, Pallas kernels, front(): pl.pallas_call(functools.partial(front_kernel, sizes=sizes, tile=min(tile...  76.2 us
    pallas_call x1, Pallas kernels, feed_forward(): pl.pallas_call(functools.partial(feed_kernel, sizes=sizes, tile=tile, gro...  75.6 us
    pallas_call x1, Pallas kernels, lay_out(): pl.pallas_call(functools.partial(lay_out_kernel, tiles=tiles), grid=(step...  8.1 us

profile of v1, /device:TPU:0, one launch (start us, length us, event | category | flops | bytes accessed | tf_op | source)
XLA Modules:
  0.0 248.2 jit_solution(15678890171886700449)
XLA Ops:
  0.6 76.2 %front.1 = (bf16[1024,1024]{1,0:T(8,128)(2,1)}, bf16[512,1024]{1,0:T(8,128)(2,1)}, bf16[6,1024,512]{2,1,0:T(8,128)(2,1)}, bf16[1024,1024]{1,0:T(8,128)(2,1)}, bf...) custom-call(s32[2]{0:T(128)} %set_ref.3, ...), custom_call_target="tpu_custom_call" | custom-call | flops 23622320128 | bytes 29360128 | tf_op jit(solution)/shard_map/front/pallas_call | solution.py:424
  76.8 75.6 %feed.1 = (bf16[1024,1024]{1,0:T(8,128)(2,1)}, f32[1024,1024]{1,0:T(8,128)}, bf16[8,1024,128]{2,1,0:T(8,128)(2,1)}, bf16[128,16,128]{2,1,0:T(8,128)(2,1)}) custom-call(s32[2]{0:T(128)} %set_ref.3, s32[2]{0:T(128)} %live_ref.1, bf16[1024,1024]{1,0:T(8,128)(2,1)} %get-tuple-element.49.x_hbm.x_ref, bf16[8,1024,128]{2,1,0:T(8,128)(2,1)} %get-tuple-element.50.att_hbm.o_ref, ...), custom_call_target="tpu_custom_call" | custom-call | flops 38654705664 | bytes 33554432 | tf_op jit(solution)/shard_map/feed/pallas_call | solution.py:951
  152.4 87.5 %back.1 = (bf16[2,512,1024]{2,1,0:T(8,128)(2,1)}, bf16[2,512,1024]{2,1,0:T(8,128)(2,1)}, bf16[32,8,3,16,128]{4,3,2,1,0:T(8,128)(2,1)}, bf16[32,8,1,16,128]{4,3,2,1,0:T(8,128)(2,1)}) custom-call(bf16[24,1024,128]{2,1,0:T(8,128)(2,1)} %get-tuple-element.48.q_ref.k_ref.v_ref, bf16[24,1024,128]{2,1,0:T(8,128)(2,1)} %get-tuple-element.48.q_ref.k_ref.v_ref, ...), custom_call_target="tpu_custom_call" | custom-call | flops 49392123904 | bytes 41943040 | tf_op jit(solution)/shard_map/back/pallas_call | solution.py:1394
  239.9 8.1 %lay_out.1 = (bf16[2,512,1024]{2,1,0:T(8,128)(2,1)}, bf16[2,512,1024]{2,1,0:T(8,128)(2,1)}, f32[8,16,1024]{2,1,0:T(8,128)}, f32[8,16,3072]{2,1,0:T(8,128)}, f32[...) custom-call(bf16[2,512,1024]{2,1,0:T(8,128)(2,1)} %get-tuple-element, ...), custom_call_target="tpu_custom_call" | custom-call | bytes 12582912 | tf_op jit(solution)/shard_map/lay_out/pallas_call | solution.py:1483
